TPU v7x, 512 devices: a whole 4x4x16 slice. The times are simulated.
512 devices in a mesh: dp: 16 (over x_hi, y, core), ctx: 32 (over x_lo, z).
Axes of the slice: x: 4 (x_hi: 2, x_lo: 2; x = x_hi * 2 + x_lo), y: 4, z: 16, core: 2. Of those that a mesh axis runs over, the one named last changes fastest.
Arguments:
- query: bfloat16 [16, 4096, 512], P('dp', 'ctx'), may hold values from -6 to 6
- key: bfloat16 [16, 4096, 512], P('dp', 'ctx'), may hold values from -6 to 6
- value: bfloat16 [16, 4096, 512], P('dp', 'ctx'), may hold values from -6 to 6
- out_grad: bfloat16 [16, 4096, 1024], P('dp', 'ctx'), may hold values from -6 to 6
- w_out: bfloat16 [512, 1024], P('dp'), may hold values from -0.25 to 0.25
- band_tiles: int32 [32, 3], replicated, may hold values from 0 to 1, as said below
- global_blocks: int32 [3], replicated, may hold values from 0 to 31, as said below
Outputs:
- query_grad: bfloat16 [16, 4096, 512], P('dp', 'ctx')
- key_grad: bfloat16 [16, 4096, 512], P('dp', 'ctx')
- value_grad: bfloat16 [16, 4096, 512], P('dp', 'ctx')
- w_out_grad: float32 [512, 1024], P(('dp', 'ctx'))
Inputs may be any that keep to these rules, and one draw needn't show every extreme that they name: band_tiles[a, c] = 1 lists the tile of query block a and key block a + c - 1; column 1 is 1 in every row; entries that point outside the utterance are ignored. `global_blocks`: distinct block numbers; 0 and 31 are among them.
All inputs are finite; a program needn't handle non-finite values.
Results may differ from a plain program's by a relative error of at most 0.03.
Values may be sent and summed in bfloat16 or wider, within the bound.
No kernel may reach another device: no remote copies, remote signals or barrier semaphores. Data moves between devices by JAX's collectives and lax.ppermute only.
A program may use at most 64 MiB of HBM per device.

v0:
```python
import jax
import jax.numpy as jnp
from jax import lax
from jax.sharding import PartitionSpec as P

HEADS = 4
HDIM = 128
BLK = 128


def padded(shard, sides, width):
    for axis, dim in sides:
        size, length = (lax.axis_size(axis), shard.shape[dim])
        up = [(i, (i + 1) % size) for i in range(size - 1)]
        down = [(j, i) for i, j in up]
        last = lax.slice_in_dim(shard, length - width, length, axis=dim)
        leading = lax.slice_in_dim(shard, 0, width, axis=dim)
        before = lax.ppermute(last, axis, up)
        after = lax.ppermute(leading, axis, down)
        shard = jnp.concatenate([before, shard, after], axis=dim)
    return shard


def from_behind(shard, axis, by):
    size = lax.axis_size(axis)
    pairs = [(i, i + by) for i in range(size) if 0 <= i + by < size]
    return lax.ppermute(shard, axis, pairs)


def tile_mask(band_tiles, global_blocks, q_first, q_count, k_first, k_count, n_blocks, band, blk):
    q_ids = q_first + jnp.arange(q_count, dtype=jnp.int32)
    k_ids = k_first + jnp.arange(k_count, dtype=jnp.int32)
    offset = k_ids[None, :] - q_ids[:, None]
    inside = (jnp.abs(offset) <= band) & (k_ids[None, :] >= 0) & (k_ids[None, :] < n_blocks)
    inside = inside & (q_ids[:, None] >= 0) & (q_ids[:, None] < n_blocks)
    table_hit = (q_ids[:, None] == jnp.arange(n_blocks, dtype=jnp.int32)[None, :]).astype(jnp.int32)
    rows_of = jnp.dot(table_hit, band_tiles)
    column = offset + band
    slots = jnp.arange(2 * band + 1, dtype=jnp.int32)
    chosen = jnp.sum(
        rows_of[:, None, :] * (column[:, :, None] == slots[None, None, :]).astype(jnp.int32), axis=2
    )
    shared = jnp.any(k_ids[:, None] == global_blocks[None, :], axis=1)
    tile = inside & (chosen > 0) & jnp.logical_not(shared)[None, :]
    full = jnp.broadcast_to(tile[:, None, :, None], (q_count, blk, k_count, blk))
    return full.reshape(q_count * blk, k_count * blk)


def contract_rows(left, right):
    return lax.dot_general(
        left, right, (((0,), (0,)), ((), ())), preferred_element_type=jnp.float32
    )


def contract_cols(left, right):
    return lax.dot_general(
        left, right, (((1,), (1,)), ((), ())), preferred_element_type=jnp.float32
    )


def on_device(query, key, value, out_grad, w_out, band_tiles, global_blocks):
    q_own = query[0]
    k_own = key[0]
    v_own = value[0]
    grad_own = out_grad[0]
    rows, width = q_own.shape
    per_dev = rows // BLK
    n_blocks = per_dev * lax.axis_size("ctx")
    first = lax.axis_index("ctx") * per_dev
    scale = HDIM ** (-0.5)
    d_out = contract_cols(grad_own, lax.all_gather(w_out, "dp", axis=0, tiled=True)).astype(
        jnp.bfloat16
    )
    pair = jnp.stack([k_own, v_own])
    wide = padded(pair, (("ctx", 1),), rows)
    local_ids = first + jnp.arange(per_dev, dtype=jnp.int32)
    pick = global_blocks[:, None] == local_ids[None, :]
    owned = jnp.einsum(
        "gb,cbrh->cgrh",
        pick.astype(jnp.bfloat16),
        pair.reshape(2, per_dev, BLK, width),
        preferred_element_type=jnp.float32,
    )
    shared = lax.psum(owned.astype(jnp.bfloat16), "ctx").reshape(2, -1, width)
    keys = jnp.concatenate([wide[0], shared[0]], 0)
    vals = jnp.concatenate([wide[1], shared[1]], 0)
    n_glob = shared.shape[1]
    band = tile_mask(
        band_tiles,
        global_blocks,
        first,
        per_dev,
        first - per_dev,
        3 * per_dev,
        n_blocks,
        per_dev,
        BLK,
    )
    mask = jnp.concatenate([band, jnp.ones((rows, n_glob), bool)], 1)
    outs, grads, key_parts, value_parts, maxima, totals, deltas = ([], [], [], [], [], [], [])
    for head in range(HEADS):
        low, high = (head * HDIM, (head + 1) * HDIM)
        q_head = q_own[:, low:high]
        k_head = keys[:, low:high]
        v_head = vals[:, low:high]
        d_head = d_out[:, low:high]
        scores = jnp.where(mask, contract_cols(q_head, k_head) * scale, -jnp.inf)
        peak = jnp.max(scores, axis=1, keepdims=True)
        expo = jnp.where(mask, jnp.exp(scores - peak), 0.0)
        total = jnp.sum(expo, axis=1, keepdims=True)
        prob = expo / total
        prob_low = prob.astype(jnp.bfloat16)
        out_head = jnp.dot(prob_low, v_head, preferred_element_type=jnp.float32).astype(
            jnp.bfloat16
        )
        delta = jnp.sum(
            d_head.astype(jnp.float32) * out_head.astype(jnp.float32), axis=1, keepdims=True
        )
        slope = contract_cols(d_head, v_head)
        dscore = (prob * (slope - delta)).astype(jnp.bfloat16)
        grads.append(
            (scale * jnp.dot(dscore, k_head, preferred_element_type=jnp.float32)).astype(
                jnp.bfloat16
            )
        )
        outs.append(out_head)
        maxima.append(peak)
        totals.append(total)
        deltas.append(delta)
        key_parts.append(scale * contract_rows(dscore, q_head))
        value_parts.append(contract_rows(prob_low, d_head))
    attended = jnp.concatenate(outs, 1)
    query_grad = jnp.concatenate(grads, 1)
    key_part = jnp.concatenate(key_parts, 1)
    value_part = jnp.concatenate(value_parts, 1)
    lower = jnp.stack([key_part[:rows], value_part[:rows]])
    upper = jnp.stack([key_part[2 * rows : 3 * rows], value_part[2 * rows : 3 * rows]])
    from_upper = from_behind(lower.astype(jnp.bfloat16), "ctx", -1).astype(lower.dtype)
    from_lower = from_behind(upper.astype(jnp.bfloat16), "ctx", 1).astype(upper.dtype)
    own = (
        jnp.stack([key_part[rows : 2 * rows], value_part[rows : 2 * rows]])
        + from_upper
        + from_lower
    )
    glob_part = jnp.stack([key_part[3 * rows :], value_part[3 * rows :]])
    glob_sum = (
        lax.psum(glob_part.astype(jnp.bfloat16), "ctx")
        .astype(jnp.float32)
        .reshape(2, -1, BLK, width)
    )
    back = jnp.einsum(
        "gb,cgrh->cbrh", pick.astype(jnp.float32), glob_sum, precision=lax.Precision.HIGHEST
    ).reshape(2, rows, width)
    summed = (own + back).astype(jnp.bfloat16)
    w_grad = lax.psum_scatter(
        contract_rows(attended, grad_own), ("dp", "ctx"), scatter_dimension=0, tiled=True
    )
    return (query_grad[None], summed[0][None], summed[1][None], w_grad)


def solution(mesh):
    return jax.shard_map(
        on_device,
        mesh=mesh,
        in_specs=(
            P("dp", "ctx", None),
            P("dp", "ctx", None),
            P("dp", "ctx", None),
            P("dp", "ctx", None),
            P("dp", None),
            P(),
            P(),
        ),
        out_specs=(
            P("dp", "ctx", None),
            P("dp", "ctx", None),
            P("dp", "ctx", None),
            P(("dp", "ctx"), None),
        ),
        check_vma=False,
    )
```

profile of v0, /device:TPU:1, one launch (start us, length us, event | category | flops | bytes accessed | tf_op | source)
XLA Modules:
  0.0 1029.6 jit_solution(11150613608643000979)
XLA Ops:
  8.1 0.9 constant_dynamic-update-slice_fusion.1
  9.0 0.9 constant_dynamic-update-slice_fusion
  10.0 0.7 compare_convert_fusion
  10.7 1.1 fusion.18
  11.9 1.3 collective-permute-start.1
  13.2 5.0 collective-permute-start
  18.9 1.1 collective-permute-done.1
  20.0 1.5 collective-permute-done
  21.6 231.9 %all-reduce.6.cloned.1.call-done = bf16[2,3,128,512]{3,2,1,0:T(8,128)(2,1)} async-done(((bf16[2,3,128,512]{3,2,1,0:T(8,128)(2,1)}), bf16[2,3,128,512]{3,2,1,0:T(8,128)(2,1)}) %all-reduce.6.cloned.1.call-update) | async-done | bytes 786448 | tf_op jit(solution)/shard_map/psum | solution.py:84
  253.5 1.2 fusion.97
  254.8 0.3 fusion.100
  255.0 0.3 fusion.99
  255.3 0.3 fusion.101
  255.6 0.3 fusion.102
  255.9 0.8 fusion.22
  256.7 1.0 convolution_convert_fusion.3
  257.7 1.0 convolution_convert_fusion.2
  258.7 1.0 convolution_convert_fusion.1
  259.8 1.7 convolution_convert_fusion
  261.5 1.0 fusion.49
  262.5 0.3 fusion.48
  262.8 0.3 fusion.47
  263.1 0.3 fusion.46
  263.5 0.3 copy-done.10
  264.0 1.0 multiply_reduce_fusion.3
  265.3 0.3 fusion.15
  266.9 0.3 fusion.13
  267.4 0.3 copy-done.4
  267.9 0.3 fusion.12
  268.5 0.8 slice_bitcast_fusion
  269.3 0.7 slice_bitcast_fusion.8
  270.1 0.8 slice_bitcast_fusion.1
  270.8 0.7 slice_bitcast_fusion.9
  271.6 0.8 copy.61
  272.3 2.1 pad_maximum_fusion.3
  274.6 1.6 pad_maximum_fusion.5
  276.2 3.1 collective-permute-start.3
  279.5 1.3 pad_maximum_fusion
  280.8 1.8 fusion.30
  282.6 0.9 copy-done.14
  283.6 1.3 collective-permute-start.2
  284.9 1.0 slice_bitcast_fusion.5
  285.9 239.5 %all-reduce.8.cloned.1.call-done = bf16[2,3,128,512]{3,2,1,0:T(8,128)(2,1)} async-done(((bf16[2,3,128,512]{3,2,1,0:T(8,128)(2,1)}), bf16[2,3,128,512]{3,2,1,0:T(8,128)(2,1)}) %all-reduce.8.cloned.1.call-update) | async-done | bytes 786448 | tf_op jit(solution)/shard_map/psum | solution.py:147
  525.4 1.9 fusion.16
  527.3 1.1 fusion.21
  528.4 0.7 fusion.98
  529.1 492.0 %all-reduce.10.cloned.1.call-done = f32[512,1024]{1,0:T(8,128)} async-done(((f32[512,1024]{1,0:T(8,128)}), f32[512,1024]{1,0:T(8,128)}) %all-reduce.10.cloned.1.call-update) | async-done | bytes 2097168
  1021.1 1.4 constant_dynamic-slice_fusion
  (106 shorter events, 4.0 us)
Async XLA Ops:
  8.0 251.8 %copy-start = (bf16[1,128,1024]{2,1,0:T(8,128)(2,1)S(1)}, bf16[1,128,1024]{2,1,0:T(8,128)(2,1)}, u32[]{:S(2)}) copy-start(bf16[1,128,1024]{2,1,0:T(8,128)(2,1)} %param.10) | copy-start | bytes 786436
  8.0 245.5 %all-reduce.6.cloned.1.call-start = ((), (), s32[]{:S(2)}) async-start(), calls=%async_computation | async-start | bytes 1572864 | tf_op jit(solution)/shard_map/psum | solution.py:84
  9.0 9.3 copy-start.34
  9.0 9.4 copy-start.24
  11.8 247.9 %all-gather.2.cloned.1.call-start = ((), (), s32[]{:S(2)}) async-start(), calls=%async_computation.1 | async-start | bytes 1114112 | tf_op jit(solution)/shard_map/all_gather | solution.py:71
  11.9 8.1 collective-permute-start.1
  13.2 8.3 collective-permute-start
  18.2 507.2 %all-reduce.8.cloned.1.call-start = ((), (), s32[]{:S(2)}) async-start(), calls=%async_computation.2 | async-start | bytes 1572864 | tf_op jit(solution)/shard_map/psum | solution.py:147
  21.6 236.1 %copy-start.9 = (bf16[384,512]{1,0:T(8,128)(2,1)}, bf16[384,512]{1,0:T(8,128)(2,1)S(1)}, u32[]{:S(2)}) copy-start(bf16[384,512]{1,0:T(8,128)(2,1)S(1)} %get-tuple-element.31) | copy-start | bytes 1179652
  21.6 233.2 %copy-start.13 = (bf16[1,128,512]{2,1,0:T(8,128)(2,1)S(1)}, bf16[1,128,512]{2,1,0:T(8,128)(2,1)}, u32[]{:S(2)}) copy-start(bf16[1,128,512]{2,1,0:T(8,128)(2,1)} %param.7) | copy-start | bytes 393220
  254.7 3.1 copy-start.11
  255.3 8.1 copy-start.3
  255.6 6.9 copy-start.5
  255.9 2.8 copy-start.25
  255.9 5.6 copy-start.7
  256.7 2.0 copy-start.28
  256.7 2.0 copy-start.30
  256.7 2.0 copy-start.32
  259.7 2.7 copy-start.31
  261.5 1.3 copy-start.29
  262.5 0.7 copy-start.27
  262.8 1.0 copy-start.10
  262.8 1.1 copy-start.12
  262.8 1.1 copy-start.17
  262.8 1.1 copy-start.19
  262.8 1.1 copy-start.21
  263.9 4.5 copy-start.1
  263.9 1.1 copy-start.8
  263.9 1.1 copy-start.26
  264.0 1.1 copy-start.33
  265.0 1.0 copy-start.6
  266.7 1.0 copy-start.4
  271.6 7.7 copy-start.2
  272.3 2.2 copy-start.16
  274.5 746.6 %all-reduce.10.cloned.1.call-start = ((), (), s32[]{:S(2)}) async-start(), calls=%async_computation.3 | async-start | bytes 4194304
  276.2 251.1 %collective-permute-start.3 = (bf16[2,128,512]{2,1,0:T(8,128)(2,1)}, bf16[2,128,512]{2,1,0:T(8,128)(2,1)}, u32[]{:S(2)}, u32[]{:S(2)}) collective-permute-start(bf16[2,128,512]{2,1,0:T(8,128)(2,1)} %pad_maximum_fusion.5), channel_id=1, source_target_pairs={{0,1},{1,2},{2,3},{3,4},{4,5},{5,6},{6,7},{7,8},{8,9},{9,10},{10,1... | collective-permute-start | bytes 786440 | tf_op jit(solution)/shard_map/ppermute | solution.py:27
  279.4 1.4 copy-start.18
  279.4 1.4 copy-start.20
  279.4 1.4 copy-start.22
  279.4 1.4 copy-start.23
  282.6 0.9 copy-start.14
  282.6 1.0 copy-start.15
  282.6 242.8 %copy-start.35 = (s32[3]{0:T(128)S(1)}, s32[3]{0:T(128)}, u32[]{:S(2)}) copy-start(s32[3]{0:T(128)} %param.13) | copy-start | bytes 40
  283.6 243.7 %collective-permute-start.2 = (bf16[2,128,512]{2,1,0:T(8,128)(2,1)S(1)}, bf16[2,128,512]{2,1,0:T(8,128)(2,1)S(1)}, u32[]{:S(2)}, u32[]{:S(2)}) collective-permute-start(bf16[2,128,512]{2,1,0:T(8,128)(2,1)S(1)} %pad_maximum_fusion.4), channel_id=1, source_target_pairs={{1,0},{2,1},{3,2},{4,3},{5,4},{6,5},{7,6},{8,7},{9,8},{10,9},{11,1... | collective-permute-start | bytes 786440 | tf_op jit(solution)/shard_map/ppermute | solution.py:27
Sparse Core Ops, SparseCore 0:
  11.9 241.5 all-reduce.5
  274.6 250.7 all-reduce.7
  530.7 490.3 all-reduce.9
Sparse Core Ops, SparseCore 1:
  18.3 65.6 all-gather.1
where the time goes:
time: 1030 us
  waiting for transfers between devices  966 us (94%)
  between operations  15.8 us (2%)
  matrix products  15.2 us (1%)
  local copies, waits for them, and re-layouts  12.2 us (1%)
  starting transfers between devices  10.9 us (1%)
    unnamed x5, waiting for transfers between devices  492 us
    psum x1, waiting for transfers between devices, on_device(): lax.psum(glob_part.astype(jnp.bfloat16), 'ctx').astype(jnp.float32)  240 us
    psum x1, waiting for transfers between devices, on_device(): shared = lax.psum(owned.astype(jnp.bfloat16), 'ctx').reshape(2, -1, width)  232 us
  transfers between devices with their start and end apart: 8, of which 5 were waited for; matrix products, arithmetic and copies ran while one was open for 2% of the time, Pallas kernels for 0%

commit v1 on v0

v1 whole, which is shorter than its diff:
```python
import jax
import jax.numpy as jnp
from jax import lax
from jax.sharding import Mesh, PartitionSpec as P

HDIM = 128
BLK = 128
HALF = 256
NZ = 16
NCTX = 32
PIECE = 8
NGLOB = 3

UP = [(i, (i + 1) % NZ) for i in range(NZ)]
DOWN = [(i, (i - 1) % NZ) for i in range(NZ)]
SWAP = [(0, 1), (1, 0)]


def by_half(*arrays):
    low = jnp.concatenate([a[:, :HALF] for a in arrays], 1)
    high = jnp.concatenate([a[:, HALF:] for a in arrays], 1)
    return low, high


def contract_rows(left, right):
    return lax.dot_general(
        left, right, (((0,), (0,)), ((), ())), preferred_element_type=jnp.float32
    )


def contract_cols(left, right):
    return lax.dot_general(
        left, right, (((1,), (1,)), ((), ())), preferred_element_type=jnp.float32
    )


def visible_blocks(band_tiles, global_blocks, block):
    seen = []
    for column in range(3):
        other = block + column - 1
        shared = jnp.any(global_blocks == other)
        inside = (other >= 0) & (other < NCTX) & (band_tiles[block, column] > 0)
        seen.append(inside & jnp.logical_not(shared))
    return jnp.stack(seen)


def on_device(query, key, value, out_grad, w_out, band_tiles, global_blocks):
    xl = lax.axis_index("xl")
    z = lax.axis_index("z")
    core = lax.axis_index("c")
    here = xl * NZ + z
    first = xl == 0
    bf16, f32 = jnp.bfloat16, jnp.float32
    scale = HDIM ** (-0.5)
    q, k, v, grad = query[0], key[0], value[0], out_grad[0]

    w_all = lax.all_gather(w_out, ("xh", "y", "c"), axis=0, tiled=True)

    kv_low, kv_high = by_half(k, v)
    kv_mine = jnp.where(first, kv_low, kv_high)
    kv_other = lax.ppermute(jnp.where(first, kv_high, kv_low), "xl", SWAP)
    q_mine = jnp.where(first, q[:, :HALF], q[:, HALF:])
    q_send = jnp.where(first, q[:, HALF:], q[:, :HALF])
    other = lax.ppermute(jnp.concatenate([q_send, grad], 1), "xl", SWAP)
    pieces = lax.all_to_all(
        jnp.stack([kv_low, kv_high]).reshape(NCTX, PIECE, 2 * HALF), ("xl", "z"), 0, 0, tiled=True
    )
    kv = jnp.stack([kv_mine, kv_other])
    before = lax.ppermute(kv, "z", UP)
    after = lax.ppermute(kv, "z", DOWN)
    before = jnp.where(z == 0, before[::-1], before)
    after = jnp.where(z == NZ - 1, after[::-1], after)
    chosen = jnp.concatenate(
        [
            lax.dynamic_index_in_dim(pieces, global_blocks[g], 0, keepdims=False)
            for g in range(NGLOB)
        ],
        0,
    )
    shared = lax.all_to_all(
        jnp.broadcast_to(chosen[None], (NZ,) + chosen.shape), "z", 0, 0, tiled=True
    ).reshape(NGLOB * BLK, 2 * HALF)

    q2 = jnp.stack([q_mine, other[:, :HALF]])
    grad2 = jnp.stack([grad, other[:, HALF:]])
    w_mine = lax.dynamic_slice_in_dim(w_all, xl * HALF, HALF, 0)
    d_out = contract_cols(grad2.reshape(2 * BLK, -1), w_mine).astype(bf16).reshape(2, BLK, HALF)

    attended, query_parts, kv_parts = [], [], []
    for slot in range(2):
        block = here if slot == 0 else (1 - xl) * NZ + z
        seen = visible_blocks(band_tiles, global_blocks, block)
        mask = jnp.concatenate([jnp.repeat(seen, BLK), jnp.ones((NGLOB * BLK,), bool)])[None]
        keys = jnp.concatenate([before[slot], kv[slot], after[slot], shared], 0)
        outs, grads, key_grads, value_grads = [], [], [], []
        for head in range(2):
            low, high = head * HDIM, (head + 1) * HDIM
            q_head = q2[slot][:, low:high]
            d_head = d_out[slot][:, low:high]
            k_head = keys[:, low:high]
            v_head = keys[:, HALF + low : HALF + high]
            scores = jnp.where(mask, contract_cols(q_head, k_head) * scale, -jnp.inf)
            peak = jnp.max(scores, axis=1, keepdims=True)
            expo = jnp.where(mask, jnp.exp(scores - peak), 0.0)
            prob = expo / jnp.sum(expo, axis=1, keepdims=True)
            prob_low = prob.astype(bf16)
            out_head = jnp.dot(prob_low, v_head, preferred_element_type=f32).astype(bf16)
            delta = jnp.sum(d_head.astype(f32) * out_head.astype(f32), axis=1, keepdims=True)
            slope = contract_cols(d_head, v_head)
            dscore = (prob * (slope - delta)).astype(bf16)
            grads.append((scale * jnp.dot(dscore, k_head, preferred_element_type=f32)).astype(bf16))
            outs.append(out_head)
            key_grads.append(scale * contract_rows(dscore, q_head))
            value_grads.append(contract_rows(prob_low, d_head))
        attended.append(jnp.concatenate(outs, 1))
        query_parts.append(jnp.concatenate(grads, 1))
        kv_parts.append(jnp.concatenate(key_grads + value_grads, 1))

    w_part = contract_rows(jnp.concatenate(attended, 0), grad2.reshape(2 * BLK, -1))
    w_part = w_part.reshape(4, 2, 2 * NZ, w_part.shape[1])
    lower = core == 0
    w_keep = jnp.where(lower, w_part[:, 0], w_part[:, 1])
    w_send = jnp.where(lower, w_part[:, 1], w_part[:, 0]).astype(bf16)
    w_sum = w_keep + lax.ppermute(w_send, "c", SWAP).astype(f32)
    w_sum = lax.all_to_all(
        w_sum.astype(bf16).reshape(8, NZ, -1), ("y", "xh"), 0, 0, tiled=True
    )
    w_sum = jnp.sum(w_sum.astype(f32), axis=0).astype(bf16).reshape(NZ, 2, 2 * HALF)

    to_lower = jnp.stack([part[:BLK] for part in kv_parts]).astype(bf16)
    to_upper = jnp.stack([part[2 * BLK : 3 * BLK] for part in kv_parts]).astype(bf16)
    to_lower = jnp.where(z == 0, to_lower[::-1], to_lower)
    to_upper = jnp.where(z == NZ - 1, to_upper[::-1], to_upper)
    from_upper = lax.ppermute(to_lower, "z", DOWN).astype(f32)
    from_lower = lax.ppermute(to_upper, "z", UP).astype(f32)
    kv_own = [kv_parts[s][BLK : 2 * BLK] + from_upper[s] + from_lower[s] for s in range(2)]
    back = lax.ppermute(
        jnp.concatenate([query_parts[1], kv_own[1].astype(bf16)], 1), "xl", SWAP
    )

    glob_part = (kv_parts[0][3 * BLK :] + kv_parts[1][3 * BLK :]).astype(bf16)
    glob_part = glob_part.reshape(NZ, NGLOB * PIECE, 2 * HALF)
    pad = jnp.zeros((NZ, PIECE - 2, 2 * HALF), bf16)
    summed = lax.all_to_all(
        jnp.concatenate([glob_part, w_sum, pad], 1), "z", 0, 0, tiled=True
    )
    summed = jnp.sum(summed.astype(f32), axis=0)
    w_row = summed[NGLOB * PIECE : NGLOB * PIECE + 2].reshape(1, 4 * HALF)
    w_row = lax.ppermute(w_row, ("xh", "xl"), [(0, 0), (1, 2), (2, 1), (3, 3)])
    glob_sum = summed[: NGLOB * PIECE].reshape(NGLOB, PIECE, 2 * HALF)
    ids = jnp.arange(NCTX, dtype=jnp.int32)[:, None, None]
    outgoing = jnp.zeros((NCTX, PIECE, 2 * HALF), f32)
    for g in range(NGLOB):
        outgoing = jnp.where(ids == global_blocks[g], glob_sum[g][None], outgoing)
    owned = lax.all_to_all(outgoing.astype(bf16), ("xl", "z"), 0, 0, tiled=True)
    owned = owned.reshape(2, BLK, 2 * HALF).astype(f32)

    q_low = jnp.where(first, query_parts[0], back[:, :HALF])
    q_high = jnp.where(first, back[:, :HALF], query_parts[0])
    kv_back = back[:, HALF:].astype(f32)
    kv_low = (jnp.where(first, kv_own[0], kv_back) + owned[0]).astype(bf16)
    kv_high = (jnp.where(first, kv_back, kv_own[0]) + owned[1]).astype(bf16)
    query_grad = jnp.concatenate([q_low, q_high], 1)
    key_grad = jnp.concatenate([kv_low[:, :HALF], kv_high[:, :HALF]], 1)
    value_grad = jnp.concatenate([kv_low[:, HALF:], kv_high[:, HALF:]], 1)
    return query_grad[None], key_grad[None], value_grad[None], w_row


def solution(mesh):
    fine = Mesh(mesh.devices.reshape(2, 4, 2, 2, NZ), ("xh", "y", "c", "xl", "z"))
    dp, ctx = ("xh", "y", "c"), ("xl", "z")
    frames = P(dp, ctx, None)
    return jax.shard_map(
        on_device,
        mesh=fine,
        in_specs=(frames, frames, frames, frames, P(dp, None), P(), P()),
        out_specs=(frames, frames, frames, P(dp + ctx, None)),
        check_vma=False,
    )
```

time: 1030 us -> 209 us (0.20)
  waiting for transfers between devices: 966 us -> 51.5 us
  starting transfers between devices: 10.9 us -> 81.1 us
  between operations: 15.8 us -> 28.4 us
  other arithmetic: 9.63 us -> 20.1 us
    unnamed x5 -> x1, waiting for transfers between devices: 492 us -> 0.68 us
    psum x2 -> x0, waiting for transfers between devices: 471 us -> none  [the longest x1 240 us: on_device(): lax.psum(glob_part.astype(jnp.bfloat16), 'ctx').astype(jnp.float32)]
    all_to_all x0 -> x5, starting transfers between devices: none -> 49.6 us  [the longest x1 16.4 us: on_device(): lax.all_to_all(jnp.stack([kv_low, kv_high]).reshape(NCTX, PIECE, 2 * HALF...]
    all_to_all x0 -> x5, waiting for transfers between devices: none -> 21.5 us  [the longest x1 9.07 us: on_device(): owned = lax.all_to_all(outgoing.astype(bf16), ('xl', 'z'), 0, 0, tiled=True)]
    ppermute x4 -> x9, starting transfers between devices: 10.7 us -> 31.5 us  [the longest x1 8.88 us: on_device(): w_sum = w_keep + lax.ppermute(w_send, 'c', SWAP).astype(f32)]
    ppermute x4 -> x9, waiting for transfers between devices: 2.53 us -> 22.9 us  [the longest x1 19.4 us: on_device(): from_lower = lax.ppermute(to_upper, 'z', UP).astype(f32)]
  transfers between devices with their start and end apart: 8 -> 15, of which waited for: 5 -> 6; matrix products, arithmetic and copies ran while one was open for 2% -> 13% of each run, Pallas kernels for 0% -> 0%
where the time goes in v1:
time: 209 us; the launch traced here: 207 us
  starting transfers between devices  81.1 us (39%)
  waiting for transfers between devices  51.5 us (25%)
  between operations  28.4 us (14%)
  other arithmetic  20.1 us (10%)
  local copies, waits for them, and re-layouts  14.5 us (7%)
  matrix products  11 us (5%)
    ppermute x1, waiting for transfers between devices, on_device(): from_lower = lax.ppermute(to_upper, 'z', UP).astype(f32)  19.4 us
    all_to_all x1, starting transfers between devices, on_device(): lax.all_to_all(jnp.stack([kv_low, kv_high]).reshape(NCTX, PIECE, 2 * HALF...  16.4 us
    all_to_all x1, starting transfers between devices, on_device(): owned = lax.all_to_all(outgoing.astype(bf16), ('xl', 'z'), 0, 0, tiled=True)  10.4 us
    all_to_all x1, starting transfers between devices, on_device(): lax.all_to_all(jnp.broadcast_to(chosen[None], (NZ,) + chosen.shape), 'z',...  10.3 us
    all_to_all x1, waiting for transfers between devices, on_device(): owned = lax.all_to_all(outgoing.astype(bf16), ('xl', 'z'), 0, 0, tiled=True)  9.07 us
    ppermute x1, starting transfers between devices, on_device(): w_sum = w_keep + lax.ppermute(w_send, 'c', SWAP).astype(f32)  8.88 us
    all_to_all x1, waiting for transfers between devices, on_device(): lax.all_to_all(jnp.broadcast_to(chosen[None], (NZ,) + chosen.shape), 'z',...  8.81 us
    all_gather x1, waiting for transfers between devices, on_device(): w_all = lax.all_gather(w_out, ('xh', 'y', 'c'), axis=0, tiled=True)  6.37 us
  transfers between devices with their start and end apart: 15, of which 6 were waited for; matrix products, arithmetic and copies ran while one was open for 13% of the time, Pallas kernels for 0%

profile of v1, /device:TPU:1, one launch (start us, length us, event | category | flops | bytes accessed | tf_op | source)
XLA Modules:
  0.0 206.6 jit_solution(18197620024677317167)
XLA Ops:
  7.2 0.7 all-gather.2.cloned.1.call-update
  7.9 1.0 copy.31
  9.1 1.0 pad_maximum_fusion.5
  10.1 3.9 %collective-permute-start.3 = (bf16[128,1280]{1,0:T(8,128)(2,1)S(1)}, bf16[128,1280]{1,0:T(8,128)(2,1)S(1)}, u32[]{:S(2)}, u32[]{:S(2)}) collective-permute-start(bf16[128,1280]{1,0:T(8,128)(2,1)S(1)} %pad_maximum_fusion.5), channel_id=1, source_target_pairs={{0,16},{16,0},{1,17},{17,1},{2,18},{18,2},{3,19},{19,3},{4,20},{20... | collective-permute-start | bytes 983048 | tf_op jit(solution)/shard_map/ppermute | solution.py:64
  14.0 1.0 copy.32
  15.4 1.9 collective-permute-start
  17.3 0.9 copy.34
  18.2 16.4 %all-to-all-start = ((bf16[32,8,512]{2,1,0:T(8,128)(2,1)}), bf16[32,8,512]{2,1,0:T(8,128)(2,1)S(1)}, u32[]{:S(2)}, u32[]{:S(2)}) async-start(bf16[32,8,512]{2,1,0:T(8,128)(2,1)} %bitcast.19), calls=%async_computation | async-start | bytes 524288 | tf_op jit(solution)/shard_map/all_to_all | solution.py:65
  34.6 0.8 compare_reduce_fusion.5
  44.4 1.3 iota_compare_fusion
  52.6 4.4 %collective-permute-start.2 = (bf16[2,128,512]{1,2,0:T(8,128)(2,1)S(1)}, bf16[2,128,512]{1,2,0:T(8,128)(2,1)S(1)}, u32[]{:S(2)}, u32[]{:S(2)}) collective-permute-start(bf16[2,128,512]{1,2,0:T(8,128)(2,1)S(1)} %pad_maximum_fusion.6), channel_id=1, source_target_pairs={{0,15},{1,0},{2,1},{3,2},{4,3},{5,4},{6,5},{7,6},{8,7},{9,8},{10,9... | collective-permute-start | bytes 786440 | tf_op jit(solution)/shard_map/ppermute | solution.py:70
  56.9 1.9 collective-permute-start.1
  59.0 0.8 broadcast_in_dim.124
  59.8 10.3 %all-to-all-start.1 = ((bf16[16,24,512]{2,1,0:T(8,128)(2,1)}), bf16[16,24,512]{2,1,0:T(8,128)(2,1)S(1)}, u32[]{:S(2)}, u32[]{:S(2)}) async-start(bf16[16,24,512]{2,1,0:T(8,128)(2,1)} %broadcast_in_dim.124), calls=%async_computation.1 | async-start | bytes 786432 | tf_op jit(solution)/shard_map/all_to_all | solution.py:80
  70.9 6.4 %all-gather.2.cloned.1.call-done = bf16[512,1024]{1,0:T(8,128)(2,1)} async-done(((bf16[32,1024]{1,0:T(8,128)(2,1)}), bf16[512,1024]{1,0:T(8,128)(2,1)}) %all-gather.2.cloned.1.call-update) | async-done | bytes 1048592 | tf_op jit(solution)/shard_map/all_gather | solution.py:57
  77.3 1.4 convolution_convert_fusion
  78.7 8.8 %all-to-all-done.1 = bf16[16,24,512]{2,1,0:T(8,128)(2,1)S(1)} async-done(((bf16[16,24,512]{2,1,0:T(8,128)(2,1)}), bf16[16,24,512]{2,1,0:T(8,128)(2,1)S(1)}, u32[]{:S(2)}, u32[]{:S(2)}) %all-to-all-start.1) | async-done | bytes 393248 | tf_op jit(solution)/shard_map/all_to_all | solution.py:80
  94.0 8.9 %collective-permute-start.7 = (bf16[4,32,1024]{2,1,0:T(8,128)(2,1)S(1)}, bf16[4,32,1024]{2,1,0:T(8,128)(2,1)S(1)}, u32[]{:S(2)}, u32[]{:S(2)}) collective-permute-start(bf16[4,32,1024]{2,1,0:T(8,128)(2,1)S(1)} %fusion.33), channel_id=1, source_target_pairs={{0,32},{32,0},{1,33},{33,1},{2,34},{34,2},{3,35},{35,3},{4,36},{36... | collective-permute-start | bytes 786440 | tf_op jit(solution)/shard_map/ppermute | solution.py:124
  104.4 0.8 fusion.19
  105.2 6.4 %all-to-all-start.2 = ((bf16[8,16,1024]{2,1,0:T(8,128)(2,1)}), bf16[8,16,1024]{2,1,0:T(8,128)(2,1)}, u32[]{:S(2)}, u32[]{:S(2)}) async-start(bf16[8,16,1024]{2,1,0:T(8,128)(2,1)} %bitcast.156), calls=%async_computation.2 | async-start | bytes 524288 | tf_op jit(solution)/shard_map/all_to_all | solution.py:125
  111.5 0.8 fusion.16
  112.4 1.9 copy.42
  114.3 2.3 %fusion.95 = bf16[768,512]{0,1:T(8,128)(2,1)} fusion(f32[768,128]{0,1:T(8,128)} %copy-done.11, f32[768,128]{0,1:T(8,128)} %copy-done.10, f32[768,128]{0,1:T(8,128)} %copy-done.1, f32[768,128]{0,1:T(8,128)} %copy-done.2), kind=kLoop, calls=%fused_computation.196 | loop fusion | flops 3145728 | bytes 2359296 | tf_op jit(solution)/shard_map/convert.10
  116.6 3.6 %all-to-all-done.2 = bf16[8,16,1024]{2,1,0:T(8,128)(2,1)} async-done(((bf16[8,16,1024]{2,1,0:T(8,128)(2,1)}), bf16[8,16,1024]{2,1,0:T(8,128)(2,1)}, u32[]{:S(2)}, u32[]{:S(2)}) %all-to-all-start.2) | async-done | bytes 262176 | tf_op jit(solution)/shard_map/all_to_all | solution.py:125
  120.2 1.6 reduce_sum.101
  121.8 1.4 reshape.165
  123.2 2.0 maximum_maximum_fusion
  125.2 6.2 %all-to-all-start.3 = ((bf16[16,32,512]{2,1,0:T(8,128)(2,1)}), bf16[16,32,512]{2,1,0:T(8,128)(2,1)}, u32[]{:S(2)}, u32[]{:S(2)}) async-start(bf16[16,32,512]{2,1,0:T(8,128)(2,1)} %maximum_maximum_fusion), calls=%async_computation.3 | async-start | bytes 1048576 | tf_op jit(solution)/shard_map/all_to_all | solution.py:144
  131.4 1.3 fusion.94
  132.7 1.0 slice_bitcast_fusion.9
  133.9 3.4 %collective-permute-start.5 = (bf16[2,128,512]{1,2,0:T(8,128)(2,1)S(1)}, bf16[2,128,512]{1,2,0:T(8,128)(2,1)S(1)}, u32[]{:S(2)}, u32[]{:S(2)}) collective-permute-start(bf16[2,128,512]{1,2,0:T(8,128)(2,1)S(1)} %reverse_select_fusion), channel_id=1, source_target_pairs={{0,1},{1,2},{2,3},{3,4},{4,5},{5,6},{6,7},{7,8},{8,9},{9,10},{10,1... | collective-permute-start | bytes 786440 | tf_op jit(solution)/shard_map/ppermute | solution.py:135
  137.3 3.3 %collective-permute-start.4 = (bf16[2,128,512]{1,2,0:T(8,128)(2,1)S(1)}, bf16[2,128,512]{1,2,0:T(8,128)(2,1)S(1)}, u32[]{:S(2)}, u32[]{:S(2)}) collective-permute-start(bf16[2,128,512]{1,2,0:T(8,128)(2,1)S(1)} %reverse_select_fusion.1), channel_id=1, source_target_pairs={{0,15},{1,0},{2,1},{3,2},{4,3},{5,4},{6,5},{7,6},{8,7},{9,8},{10,9... | collective-permute-start | bytes 786440 | tf_op jit(solution)/shard_map/ppermute | solution.py:134
  140.6 1.8 fusion.12
  143.0 19.4 %collective-permute-done.5 = bf16[2,128,512]{1,2,0:T(8,128)(2,1)S(1)} collective-permute-done((bf16[2,128,512]{1,2,0:T(8,128)(2,1)S(1)}, bf16[2,128,512]{1,2,0:T(8,128)(2,1)S(1)}, u32[]{:S(2)}, u32[]{:S(2)}) %collective-permute-start.5) | collective-permute-done | bytes 262176 | tf_op jit(solution)/shard_map/ppermute | solution.py:135
  162.4 0.8 convert_element_type.148
  163.3 0.8 convert_element_type.147
  164.1 1.1 convert_reduce_fusion
  165.3 0.9 select_convert_fusion
  166.2 10.4 %all-to-all-start.4 = ((bf16[32,8,512]{2,1,0:T(8,128)(2,1)}), bf16[32,8,512]{2,1,0:T(8,128)(2,1)S(1)}, u32[]{:S(2)}, u32[]{:S(2)}) async-start(bf16[32,8,512]{2,1,0:T(8,128)(2,1)} %select_convert_fusion), calls=%async_computation.4 | async-start | bytes 524288 | tf_op jit(solution)/shard_map/all_to_all | solution.py:155
  176.5 1.1 fusion.37
  177.6 3.1 %collective-permute-start.6 = (bf16[128,768]{0,1:T(8,128)(2,1)S(1)}, bf16[128,768]{0,1:T(8,128)(2,1)S(1)}, u32[]{:S(2)}, u32[]{:S(2)}) collective-permute-start(bf16[128,768]{0,1:T(8,128)(2,1)S(1)} %pad_maximum_fusion.10), channel_id=1, source_target_pairs={{0,16},{16,0},{1,17},{17,1},{2,18},{18,2},{3,19},{19,3},{4,20},{20... | collective-permute-start | bytes 589832 | tf_op jit(solution)/shard_map/ppermute | solution.py:137
  180.8 1.3 fusion.13
  182.1 3.5 %collective-permute-done.6 = bf16[128,768]{0,1:T(8,128)(2,1)S(1)} collective-permute-done((bf16[128,768]{0,1:T(8,128)(2,1)S(1)}, bf16[128,768]{0,1:T(8,128)(2,1)S(1)}, u32[]{:S(2)}, u32[]{:S(2)}) %collective-permute-start.6) | collective-permute-done | bytes 196640 | tf_op jit(solution)/shard_map/ppermute | solution.py:137
  186.4 0.8 copy.49
  187.1 9.1 %all-to-all-done.4 = bf16[32,8,512]{2,1,0:T(8,128)(2,1)S(1)} async-done(((bf16[32,8,512]{2,1,0:T(8,128)(2,1)}), bf16[32,8,512]{2,1,0:T(8,128)(2,1)S(1)}, u32[]{:S(2)}, u32[]{:S(2)}) %all-to-all-start.4) | async-done | bytes 262176 | tf_op jit(solution)/shard_map/all_to_all | solution.py:155
  196.6 1.0 fusion.30
  197.6 0.8 copy.51
  198.4 0.8 copy.50
  (144 shorter events, 13.9 us)
Async XLA Ops:
  7.2 7.9 %copy-start.21 = (bf16[1,128,512]{2,1,0:T(8,128)(2,1)S(1)}, bf16[1,128,512]{2,1,0:T(8,128)(2,1)}, u32[]{:S(2)}) copy-start(bf16[1,128,512]{2,1,0:T(8,128)(2,1)} %param.9) | copy-start | bytes 393220
  7.2 70.1 %all-gather.2.cloned.1.call-start = ((), (), s32[]{:S(2)}) async-start(), calls=%async_computation.5 | async-start | bytes 1114112 | tf_op jit(solution)/shard_map/all_gather | solution.py:57
  10.1 60.1 %collective-permute-start.3 = (bf16[128,1280]{1,0:T(8,128)(2,1)S(1)}, bf16[128,1280]{1,0:T(8,128)(2,1)S(1)}, u32[]{:S(2)}, u32[]{:S(2)}) collective-permute-start(bf16[128,1280]{1,0:T(8,128)(2,1)S(1)} %pad_maximum_fusion.5), channel_id=1, source_target_pairs={{0,16},{16,0},{1,17},{17,1},{2,18},{18,2},{3,19},{19,3},{4,20},{20... | collective-permute-start | bytes 983048 | tf_op jit(solution)/shard_map/ppermute | solution.py:64
  15.2 19.4 %copy-start.23 = (s32[3]{0:T(128)S(1)}, s32[3]{0:T(128)}, u32[]{:S(2)}) copy-start(s32[3]{0:T(128)} %param.13) | copy-start | bytes 40
  15.2 24.4 %copy-start.24 = (s32[32,3]{0,1:T(4,128)S(1)}, s32[32,3]{0,1:T(4,128)}, u32[]{:S(2)}) copy-start(s32[32,3]{0,1:T(4,128)} %param.12) | copy-start | bytes 1156
  15.4 37.1 %collective-permute-start = (bf16[128,512]{0,1:T(8,128)(2,1)S(1)}, bf16[128,512]{0,1:T(8,128)(2,1)S(1)}, u32[]{:S(2)}, u32[]{:S(2)}) collective-permute-start(bf16[128,512]{0,1:T(8,128)(2,1)S(1)} %get-tuple-element.41), channel_id=1, source_target_pairs={{0,16},{16,0},{1,17},{17,1},{2,18},{18,2},{3,19},{19,3},{4,20},{20... | collective-permute-start | bytes 393224 | tf_op jit(solution)/shard_map/ppermute | solution.py:61
  18.2 40.8 %all-to-all-start = ((bf16[32,8,512]{2,1,0:T(8,128)(2,1)}), bf16[32,8,512]{2,1,0:T(8,128)(2,1)S(1)}, u32[]{:S(2)}, u32[]{:S(2)}) async-start(bf16[32,8,512]{2,1,0:T(8,128)(2,1)} %bitcast.19), calls=%async_computation | async-start | bytes 524288 | tf_op jit(solution)/shard_map/all_to_all | solution.py:65
  50.4 19.8 %copy-start.12 = (bf16[1,128,1024]{2,1,0:T(8,128)(2,1)S(1)}, bf16[1,128,1024]{2,1,0:T(8,128)(2,1)}, u32[]{:S(2)}) copy-start(bf16[1,128,1024]{2,1,0:T(8,128)(2,1)} %param.10) | copy-start | bytes 786436
  52.6 17.7 %collective-permute-start.2 = (bf16[2,128,512]{1,2,0:T(8,128)(2,1)S(1)}, bf16[2,128,512]{1,2,0:T(8,128)(2,1)S(1)}, u32[]{:S(2)}, u32[]{:S(2)}) collective-permute-start(bf16[2,128,512]{1,2,0:T(8,128)(2,1)S(1)} %pad_maximum_fusion.6), channel_id=1, source_target_pairs={{0,15},{1,0},{2,1},{3,2},{4,3},{5,4},{6,5},{7,6},{8,7},{9,8},{10,9... | collective-permute-start | bytes 786440 | tf_op jit(solution)/shard_map/ppermute | solution.py:70
  56.9 13.7 %collective-permute-start.1 = (bf16[2,128,512]{1,2,0:T(8,128)(2,1)S(1)}, bf16[2,128,512]{1,2,0:T(8,128)(2,1)S(1)}, u32[]{:S(2)}, u32[]{:S(2)}) collective-permute-start(bf16[2,128,512]{1,2,0:T(8,128)(2,1)S(1)} %pad_maximum_fusion.6), channel_id=1, source_target_pairs={{0,1},{1,2},{2,3},{3,4},{4,5},{5,6},{6,7},{7,8},{8,9},{9,10},{10,1... | collective-permute-start | bytes 786440 | tf_op jit(solution)/shard_map/ppermute | solution.py:69
  59.8 27.7 %all-to-all-start.1 = ((bf16[16,24,512]{2,1,0:T(8,128)(2,1)}), bf16[16,24,512]{2,1,0:T(8,128)(2,1)S(1)}, u32[]{:S(2)}, u32[]{:S(2)}) async-start(bf16[16,24,512]{2,1,0:T(8,128)(2,1)} %broadcast_in_dim.124), calls=%async_computation.1 | async-start | bytes 786432 | tf_op jit(solution)/shard_map/all_to_all | solution.py:80
  87.6 4.8 %copy-start.3 = (bf16[768,512]{1,0:T(8,128)(2,1)}, bf16[768,512]{1,0:T(8,128)(2,1)S(1)}, u32[]{:S(2)}) copy-start(bf16[768,512]{1,0:T(8,128)(2,1)S(1)} %get-tuple-element.34) | copy-start | bytes 2359300
  87.6 5.8 %copy-start.4 = (bf16[768,512]{1,0:T(8,128)(2,1)}, bf16[768,512]{1,0:T(8,128)(2,1)S(1)}, u32[]{:S(2)}) copy-start(bf16[768,512]{1,0:T(8,128)(2,1)S(1)} %get-tuple-element.35) | copy-start | bytes 2359300
  89.2 14.4 %copy-start.8 = (f32[768,128]{0,1:T(8,128)}, f32[768,128]{0,1:T(8,128)S(1)}, u32[]{:S(2)}) copy-start(f32[768,128]{0,1:T(8,128)S(1)} %fusion.61) | copy-start | bytes 1179652
  90.8 12.7 %copy-start.10 = (f32[768,128]{0,1:T(8,128)}, f32[768,128]{0,1:T(8,128)S(1)}, u32[]{:S(2)}) copy-start(f32[768,128]{0,1:T(8,128)S(1)} %fusion.58) | copy-start | bytes 1179652
  91.5 12.0 %copy-start.11 = (f32[768,128]{0,1:T(8,128)}, f32[768,128]{0,1:T(8,128)S(1)}, u32[]{:S(2)}) copy-start(f32[768,128]{0,1:T(8,128)S(1)} %fusion.55) | copy-start | bytes 1179652
  91.8 11.8 %copy-start.9 = (f32[768,128]{0,1:T(8,128)}, f32[768,128]{0,1:T(8,128)S(1)}, u32[]{:S(2)}) copy-start(f32[768,128]{0,1:T(8,128)S(1)} %fusion.64) | copy-start | bytes 1179652
  92.4 0.7 copy-start.13
  92.7 0.7 copy-start.14
  93.1 10.5 %copy-start = (f32[768,128]{0,1:T(8,128)}, f32[768,128]{0,1:T(8,128)S(1)}, u32[]{:S(2)}) copy-start(f32[768,128]{0,1:T(8,128)S(1)} %convolution_multiply_fusion.1) | copy-start | bytes 1179652
  93.4 9.8 %copy-start.16 = (bf16[128,768]{1,0:T(8,128)(2,1)}, bf16[128,768]{1,0:T(8,128)(2,1)S(1)}, u32[]{:S(2)}) copy-start(bf16[128,768]{1,0:T(8,128)(2,1)S(1)} %fusion.9) | copy-start | bytes 589828
  93.7 9.3 %copy-start.18 = (bf16[128,768]{1,0:T(8,128)(2,1)}, bf16[128,768]{1,0:T(8,128)(2,1)S(1)}, u32[]{:S(2)}) copy-start(bf16[128,768]{1,0:T(8,128)(2,1)S(1)} %fusion.8) | copy-start | bytes 589828
  94.0 10.3 %collective-permute-start.7 = (bf16[4,32,1024]{2,1,0:T(8,128)(2,1)S(1)}, bf16[4,32,1024]{2,1,0:T(8,128)(2,1)S(1)}, u32[]{:S(2)}, u32[]{:S(2)}) collective-permute-start(bf16[4,32,1024]{2,1,0:T(8,128)(2,1)S(1)} %fusion.33), channel_id=1, source_target_pairs={{0,32},{32,0},{1,33},{33,1},{2,34},{34,2},{3,35},{35,3},{4,36},{36... | collective-permute-start | bytes 786440 | tf_op jit(solution)/shard_map/ppermute | solution.py:124
  103.2 0.8 copy-start.1
  103.5 0.7 copy-start.2
  105.2 15.0 %all-to-all-start.2 = ((bf16[8,16,1024]{2,1,0:T(8,128)(2,1)}), bf16[8,16,1024]{2,1,0:T(8,128)(2,1)}, u32[]{:S(2)}, u32[]{:S(2)}) async-start(bf16[8,16,1024]{2,1,0:T(8,128)(2,1)} %bitcast.156), calls=%async_computation.2 | async-start | bytes 524288 | tf_op jit(solution)/shard_map/all_to_all | solution.py:125
  125.2 38.9 %all-to-all-start.3 = ((bf16[16,32,512]{2,1,0:T(8,128)(2,1)}), bf16[16,32,512]{2,1,0:T(8,128)(2,1)}, u32[]{:S(2)}, u32[]{:S(2)}) async-start(bf16[16,32,512]{2,1,0:T(8,128)(2,1)} %maximum_maximum_fusion), calls=%async_computation.3 | async-start | bytes 1048576 | tf_op jit(solution)/shard_map/all_to_all | solution.py:144
  132.7 7.9 %copy-start.15 = (bf16[128,768]{1,0:T(8,128)(2,1)S(1)}, bf16[128,768]{1,0:T(8,128)(2,1)}, u32[]{:S(2)}) copy-start(bf16[128,768]{1,0:T(8,128)(2,1)} %copy-done.14) | copy-start | bytes 589828
  133.7 8.7 %copy-start.5 = (bf16[768,512]{1,0:T(8,128)(2,1)S(1)}, bf16[768,512]{1,0:T(8,128)(2,1)}, u32[]{:S(2)}) copy-start(bf16[768,512]{1,0:T(8,128)(2,1)} %copy-done.4) | copy-start | bytes 2359300
  133.7 8.7 %copy-start.17 = (bf16[128,768]{1,0:T(8,128)(2,1)S(1)}, bf16[128,768]{1,0:T(8,128)(2,1)}, u32[]{:S(2)}) copy-start(bf16[128,768]{1,0:T(8,128)(2,1)} %copy-done.16) | copy-start | bytes 589828
  133.8 9.0 %copy-start.19 = (bf16[128,768]{1,0:T(8,128)(2,1)S(1)}, bf16[128,768]{1,0:T(8,128)(2,1)}, u32[]{:S(2)}) copy-start(bf16[128,768]{1,0:T(8,128)(2,1)} %copy-done.18) | copy-start | bytes 589828
  133.9 28.6 %collective-permute-start.5 = (bf16[2,128,512]{1,2,0:T(8,128)(2,1)S(1)}, bf16[2,128,512]{1,2,0:T(8,128)(2,1)S(1)}, u32[]{:S(2)}, u32[]{:S(2)}) collective-permute-start(bf16[2,128,512]{1,2,0:T(8,128)(2,1)S(1)} %reverse_select_fusion), channel_id=1, source_target_pairs={{0,1},{1,2},{2,3},{3,4},{4,5},{5,6},{6,7},{7,8},{8,9},{9,10},{10,1... | collective-permute-start | bytes 786440 | tf_op jit(solution)/shard_map/ppermute | solution.py:135
  137.3 26.0 %collective-permute-start.4 = (bf16[2,128,512]{1,2,0:T(8,128)(2,1)S(1)}, bf16[2,128,512]{1,2,0:T(8,128)(2,1)S(1)}, u32[]{:S(2)}, u32[]{:S(2)}) collective-permute-start(bf16[2,128,512]{1,2,0:T(8,128)(2,1)S(1)} %reverse_select_fusion.1), channel_id=1, source_target_pairs={{0,15},{1,0},{2,1},{3,2},{4,3},{5,4},{6,5},{7,6},{8,7},{9,8},{10,9... | collective-permute-start | bytes 786440 | tf_op jit(solution)/shard_map/ppermute | solution.py:134
  166.2 30.0 %all-to-all-start.4 = ((bf16[32,8,512]{2,1,0:T(8,128)(2,1)}), bf16[32,8,512]{2,1,0:T(8,128)(2,1)S(1)}, u32[]{:S(2)}, u32[]{:S(2)}) async-start(bf16[32,8,512]{2,1,0:T(8,128)(2,1)} %select_convert_fusion), calls=%async_computation.4 | async-start | bytes 524288 | tf_op jit(solution)/shard_map/all_to_all | solution.py:155
  176.5 9.1 %copy-start.22 = (bf16[128,128]{0,1:T(8,128)(2,1)S(1)}, bf16[128,128]{0,1:T(8,128)(2,1)}, u32[]{:S(2)}) copy-start(bf16[128,128]{0,1:T(8,128)(2,1)} %fusion.12) | copy-start | bytes 98308
  177.6 7.9 %collective-permute-start.6 = (bf16[128,768]{0,1:T(8,128)(2,1)S(1)}, bf16[128,768]{0,1:T(8,128)(2,1)S(1)}, u32[]{:S(2)}, u32[]{:S(2)}) collective-permute-start(bf16[128,768]{0,1:T(8,128)(2,1)S(1)} %pad_maximum_fusion.10), channel_id=1, source_target_pairs={{0,16},{16,0},{1,17},{17,1},{2,18},{18,2},{3,19},{19,3},{4,20},{20... | collective-permute-start | bytes 589832 | tf_op jit(solution)/shard_map/ppermute | solution.py:137
  185.6 10.6 %copy-start.20 = (bf16[128,768]{0,1:T(8,128)(2,1)}, bf16[128,768]{0,1:T(8,128)(2,1)S(1)}, u32[]{:S(2)}) copy-start(bf16[128,768]{0,1:T(8,128)(2,1)S(1)} %collective-permute-done.6) | copy-start | bytes 589828
  185.7 1.5 collective-permute-start.8
  186.3 10.2 %copy-start.6 = (f32[2,128,512]{1,2,0:T(8,128)S(1)}, f32[2,128,512]{1,2,0:T(8,128)}, u32[]{:S(2)}) copy-start(f32[2,128,512]{1,2,0:T(8,128)} %convert_element_type.148) | copy-start | bytes 1572868
  186.4 10.2 %copy-start.7 = (f32[2,128,512]{1,2,0:T(8,128)S(1)}, f32[2,128,512]{1,2,0:T(8,128)}, u32[]{:S(2)}) copy-start(f32[2,128,512]{1,2,0:T(8,128)} %convert_element_type.147) | copy-start | bytes 1572868
Sparse Core Ops, SparseCore 0:
  11.3 65.9 all-gather.1

commit v2 on v1

v2 whole, which is shorter than its diff:
```python
import jax
import jax.numpy as jnp
from jax import lax
from jax.experimental import pallas as pl
from jax.experimental.pallas import tpu as pltpu
from jax.sharding import Mesh, PartitionSpec as P

HDIM = 128
BLK = 128
HALF = 256
NZ = 16
NY = 4
NCTX = 32
PIECE = 8
NGLOB = 3
DM = 1024
SCALE = HDIM ** (-0.5)

UP = [(i, (i + 1) % NZ) for i in range(NZ)]
DOWN = [(i, (i - 1) % NZ) for i in range(NZ)]
SWAP = [(0, 1), (1, 0)]
CROSS = [(0, 0), (1, 2), (2, 1), (3, 3)]
Y_ONE = [(i, i ^ 1) for i in range(NY)]
Y_TWO = [(i, i ^ 2) for i in range(NY)]

VMEM = pl.BlockSpec(memory_space=pltpu.VMEM)
SMEM = pl.BlockSpec(memory_space=pltpu.SMEM)
ANY = pl.BlockSpec(memory_space=pl.ANY)
BF16, F32 = jnp.bfloat16, jnp.float32


def shaped(shape, dtype=BF16):
    return jax.ShapeDtypeStruct(shape, dtype)


def call(kernel, specs, operands, out_shape, scratch=(), flops=0, nbytes=2**20):
    return pl.pallas_call(
        kernel,
        out_shape=out_shape,
        in_specs=specs,
        out_specs=jax.tree.map(lambda _: VMEM, out_shape),
        scratch_shapes=scratch,
        compiler_params=pltpu.CompilerParams(vmem_limit_bytes=32 * 2**20),
        cost_estimate=pl.CostEstimate(flops=flops, bytes_accessed=nbytes, transcendentals=0),
    )(*operands)


def rows_dot(left, right):
    return lax.dot_general(left, right, (((0,), (0,)), ((), ())), preferred_element_type=F32)


def cols_dot(left, right):
    return lax.dot_general(left, right, (((1,), (1,)), ((), ())), preferred_element_type=F32)


def shard_rows(i, j):
    y = lax.axis_index("y") ^ i
    core = lax.axis_index("c") ^ j
    return pl.ds(pl.multiple_of((y * 2 + core) * NCTX, NCTX), NCTX)


def split_kernel(q_hbm, k_hbm, v_hbm, halves_ref, mine_ref, send_ref, parts, sems):
    first = lax.axis_index("xl") == 0
    copies = [
        pltpu.make_async_copy(ref, parts.at[i], sems.at[i])
        for i, ref in enumerate((k_hbm, v_hbm, q_hbm))
    ]
    for copy in copies:
        copy.start()
    for part in range(3):
        copies[part].wait()
        ref = parts.at[part]
        low, high = ref[:, :HALF], ref[:, HALF:]
        lanes = slice(part * HALF, (part + 1) * HALF)
        if part < 2:
            halves_ref[0, :, lanes] = low
            halves_ref[1, :, lanes] = high
        mine_ref[:, lanes] = jnp.where(first, low, high)
        send_ref[:, lanes] = jnp.where(first, high, low)


def stack_kernel(mine_ref, other_ref, kv_ref):
    kv_ref[0] = mine_ref[:, : 2 * HALF]
    kv_ref[1] = other_ref[:, : 2 * HALF]


def choose_kernel(globals_ref, pieces_ref, *refs):
    chosen_ref = refs[-1]
    for g in range(NGLOB):
        piece = pieces_ref[globals_ref[g]]
        for z in range(NZ):
            chosen_ref[z, :, g * 2 * HALF : (g + 1) * 2 * HALF] = piece


def project_kernel(w_ref, w_other_ref, grad_ref, grad_other_ref, d_ref, d_other_ref, w_scr):
    for j, ref in enumerate((w_ref, w_other_ref)):
        for i in range(NY):
            w_scr[shard_rows(i, j)] = ref[i * NCTX : (i + 1) * NCTX]
    d_ref[...] = cols_dot(grad_ref[...], w_scr[...]).astype(BF16)
    d_other_ref[...] = cols_dot(grad_other_ref[...], w_scr[...]).astype(BF16)


def attention_kernel(
    tiles_ref, globals_ref, mine_ref, other_ref, before_ref, after_ref, shared_ref,
    d_mine_ref, d_other_ref, grad_ref, grad_other_ref,
    dq_ref, own_ref, lower_ref, upper_ref, glob_ref, keep_ref, send_ref, attended_ref,
    projected_ref,
):
    xl = lax.axis_index("xl")
    z = lax.axis_index("z")
    for slot in range(2):
        block = (xl if slot == 0 else 1 - xl) * NZ + z
        kvq_ref = mine_ref if slot == 0 else other_ref
        d_ref = d_mine_ref if slot == 0 else d_other_ref
        below = jnp.where(z == 0, 1 - slot, slot)
        above = jnp.where(z == NZ - 1, 1 - slot, slot)
        seen = []
        for column in range(3):
            other = block + column - 1
            is_global = other == globals_ref[0]
            for g in range(1, NGLOB):
                is_global = is_global | (other == globals_ref[g])
            listed = tiles_ref[block, column] > 0
            seen.append((other >= 0) & (other < NCTX) & listed & jnp.logical_not(is_global))
        chunk = lax.broadcasted_iota(jnp.int32, (1, 6 * BLK), 1) // BLK
        mask = chunk >= 3
        for column in range(3):
            mask = mask | ((chunk == column) & seen[column])
        for head in range(2):
            lanes = slice(head * HDIM, (head + 1) * HDIM)
            v_lanes = slice(HALF + head * HDIM, HALF + (head + 1) * HDIM)
            q_lanes = slice(2 * HALF + head * HDIM, 2 * HALF + (head + 1) * HDIM)
            q_head = kvq_ref[:, q_lanes]
            d_head = d_ref[:, lanes]

            def gathered(at):
                parts = [before_ref[below, :, at], kvq_ref[:, at], after_ref[above, :, at]]
                for g in range(NGLOB):
                    start = g * 2 * HALF + at.start
                    parts.append(shared_ref[:, start : start + HDIM])
                return jnp.concatenate(parts, 0)

            keys, vals = gathered(lanes), gathered(v_lanes)
            scores = jnp.where(mask, cols_dot(q_head, keys) * SCALE, -jnp.inf)
            peak = jnp.max(scores, axis=1, keepdims=True)
            expo = jnp.exp(scores - peak)
            prob = expo / jnp.sum(expo, axis=1, keepdims=True)
            prob_low = prob.astype(BF16)
            out = jnp.dot(prob_low, vals, preferred_element_type=F32).astype(BF16)
            attended_ref[slot * BLK : (slot + 1) * BLK, lanes] = out
            delta = jnp.sum(d_head.astype(F32) * out.astype(F32), axis=1, keepdims=True)
            dscore = (prob * (cols_dot(d_head, vals) - delta)).astype(BF16)
            dq = SCALE * jnp.dot(dscore, keys, preferred_element_type=F32)
            dq_ref[slot, :, lanes] = dq.astype(BF16)
            for at, grad in (
                (lanes, SCALE * rows_dot(dscore, q_head)),
                (v_lanes, rows_dot(prob_low, d_head)),
            ):
                lower_ref[below, :, at] = grad[:BLK].astype(BF16)
                own_ref[slot, :, at] = grad[BLK : 2 * BLK]
                upper_ref[above, :, at] = grad[2 * BLK : 3 * BLK].astype(BF16)
                for g in range(NGLOB):
                    start = g * 2 * HALF + at.start
                    part = grad[(3 + g) * BLK : (4 + g) * BLK]
                    if slot == 0:
                        glob_ref[:, start : start + HDIM] = part
                    else:
                        glob_ref[:, start : start + HDIM] += part
    projected_ref[...] = rows_dot(attended_ref[:BLK], grad_ref[...])
    projected_ref[...] += rows_dot(attended_ref[BLK:], grad_other_ref[...])
    for i in range(NY):
        keep_ref[i] = projected_ref[shard_rows(i, 0)]
        send_ref[i] = projected_ref[shard_rows(i, 1)].astype(BF16)


def attention_call(*operands):
    def kernel(*refs):
        ins, outs, scratch = refs[:11], refs[11:18], refs[18:]
        glob_out, rest = outs[4], scratch
        attention_kernel(*ins, *outs[:4], rest[0], outs[5], outs[6], rest[1], rest[2])
        glob_out[...] = rest[0][...].astype(BF16)

    out_shape = (
        shaped((2, BLK, HALF)),
        shaped((2, BLK, 2 * HALF), F32),
        shaped((2, BLK, 2 * HALF)),
        shaped((2, BLK, 2 * HALF)),
        shaped((BLK, NGLOB * 2 * HALF)),
        shaped((NY, NCTX, DM), F32),
        shaped((NY, NCTX, DM)),
    )
    return pl.pallas_call(
        kernel,
        out_shape=out_shape,
        in_specs=[SMEM] * 2 + [VMEM] * 9,
        out_specs=(VMEM,) * len(out_shape),
        scratch_shapes=[
            pltpu.VMEM((BLK, NGLOB * 2 * HALF), F32),
            pltpu.VMEM((2 * BLK, HALF), BF16),
            pltpu.VMEM((HALF, DM), F32),
        ],
        compiler_params=pltpu.CompilerParams(vmem_limit_bytes=32 * 2**20),
        cost_estimate=pl.CostEstimate(
            flops=10**9, bytes_accessed=5 * 2**20, transcendentals=400000
        ),
    )(*operands)


def final_kernel(dq_ref, own_ref, upper_ref, lower_ref, back_ref, owned_ref, q_ref, k_ref, v_ref):
    first = lax.axis_index("xl") == 0
    own = own_ref[0] + upper_ref[0].astype(F32) + lower_ref[0].astype(F32)
    for half in range(2):
        mine = first if half == 0 else jnp.logical_not(first)
        back = back_ref[:, HALF:].astype(F32)
        owned = owned_ref[half * BLK : (half + 1) * BLK, : 2 * HALF].astype(F32)
        kv = (jnp.where(mine, own, back) + owned).astype(BF16)
        lanes = slice(half * HALF, (half + 1) * HALF)
        k_ref[:, lanes] = kv[:, :HALF]
        v_ref[:, lanes] = kv[:, HALF:]
        q_ref[:, lanes] = jnp.where(mine, dq_ref[0], back_ref[:, :HALF])


def on_device(query, key, value, out_grad, w_out, band_tiles, global_blocks):
    xl = lax.axis_index("xl")
    q, k, v, grad = query[0], key[0], value[0], out_grad[0]

    halves, mine, send = call(
        split_kernel,
        [ANY] * 3,
        (q, k, v),
        (shaped((2, BLK, 2 * HALF)), shaped((BLK, 3 * HALF)), shaped((BLK, 3 * HALF))),
        [pltpu.VMEM((3, BLK, 2 * HALF), BF16), pltpu.SemaphoreType.DMA((3,))],
    )
    pieces = lax.all_to_all(
        halves.reshape(NCTX, PIECE, 2 * HALF), ("xl", "z"), 0, 0, tiled=True
    )
    other = lax.ppermute(send, "xl", SWAP)
    w0 = lax.ppermute(w_out, ("xh", "xl"), CROSS)
    kv = call(stack_kernel, [VMEM] * 2, (mine, other), shaped((2, BLK, 2 * HALF)))
    before = lax.ppermute(kv, "z", UP)
    after = lax.ppermute(kv, "z", DOWN)
    w1 = lax.ppermute(w0, "y", Y_ONE)
    grad_other = lax.ppermute(grad, "xl", SWAP)
    chosen = call(
        choose_kernel,
        [SMEM, VMEM] + [ANY] * 4,
        (global_blocks, pieces, before, after, w1, grad_other),
        shaped((NZ, PIECE, NGLOB * 2 * HALF)),
    )
    shared = lax.all_to_all(chosen, "z", 0, 0, tiled=True).reshape(BLK, NGLOB * 2 * HALF)
    w01 = jnp.concatenate([w0, w1], 0)
    w_core = jnp.concatenate([w01, lax.ppermute(w01, "y", Y_TWO)], 0)
    d_mine, d_other = call(
        project_kernel,
        [VMEM] * 4,
        (w_core, lax.ppermute(w_core, "c", SWAP), grad, grad_other),
        (shaped((BLK, HALF)), shaped((BLK, HALF))),
        [pltpu.VMEM((HALF, DM), BF16)],
    )

    dq, own, to_lower, to_upper, glob, w_keep, w_send = attention_call(
        band_tiles, global_blocks, mine, other, before, after, shared,
        d_mine, d_other, grad, grad_other,
    )

    glob = lax.all_to_all(
        glob.reshape(NZ, PIECE, NGLOB * 2 * HALF), "z", 0, 0, tiled=True
    )
    w_sum = w_keep + lax.ppermute(w_send, "c", SWAP).astype(F32)
    w_sum = w_sum[:2] + lax.ppermute(w_sum[2:].astype(BF16), "y", Y_TWO).astype(F32)
    w_sum = w_sum[0] + lax.ppermute(w_sum[1].astype(BF16), "y", Y_ONE).astype(F32)
    w_sum += lax.ppermute(w_sum.astype(BF16), "xh", SWAP).astype(F32)
    w_sum = jnp.where(lax.axis_index("xh") == xl, w_sum, 0.0).astype(BF16)
    w_sum = w_sum.reshape(NCTX, PIECE, DM // PIECE)

    from_upper = lax.ppermute(to_lower, "z", DOWN)
    from_lower = lax.ppermute(to_upper, "z", UP)
    kv_other = own[1] + from_upper[1].astype(F32) + from_lower[1].astype(F32)
    back = lax.ppermute(jnp.concatenate([dq[1], kv_other.astype(BF16)], 1), "xl", SWAP)

    glob = jnp.sum(glob.astype(F32), axis=0).astype(BF16)
    ids = jnp.arange(NCTX, dtype=jnp.int32)[:, None, None]
    outgoing = jnp.zeros((NCTX, PIECE, 2 * HALF), BF16)
    for g in range(NGLOB):
        part = glob[None, :, g * 2 * HALF : (g + 1) * 2 * HALF]
        outgoing = jnp.where(ids == global_blocks[g], part, outgoing)
    owned = lax.all_to_all(
        jnp.concatenate([outgoing, w_sum], 2), ("xl", "z"), 0, 0, tiled=True
    )
    w_row = jnp.sum(owned[:, :, 2 * HALF :].astype(F32), axis=0).reshape(1, DM)
    full = shaped((BLK, 2 * HALF))
    query_grad, key_grad, value_grad = call(
        final_kernel,
        [VMEM] * 6,
        (dq, own, from_upper, from_lower, back, owned.reshape(2 * BLK, -1)),
        (full, full, full),
    )
    return query_grad[None], key_grad[None], value_grad[None], w_row


def solution(mesh):
    fine = Mesh(mesh.devices.reshape(2, NY, 2, 2, NZ), ("xh", "y", "c", "xl", "z"))
    dp, ctx = ("xh", "y", "c"), ("xl", "z")
    frames = P(dp, ctx, None)
    return jax.shard_map(
        on_device,
        mesh=fine,
        in_specs=(frames, frames, frames, frames, P(dp, None), P(), P()),
        out_specs=(frames, frames, frames, P(dp + ctx, None)),
        check_vma=False,
    )
```

time: 209 us -> 164 us (0.78)
  starting transfers between devices: 81.1 us -> 112 us
  between operations: 28.4 us -> 1.07 us
  waiting for transfers between devices: 51.5 us -> 31 us
  other arithmetic: 20.1 us -> 3.77 us
  matrix products: 11 us -> 0 us
  local copies, waits for them, and re-layouts: 14.5 us -> 4.88 us
  Pallas kernels: 0 us -> 8.88 us
    ppermute x7 -> x13, starting transfers between devices: 25.2 us -> 57.6 us  [the longest x1 9.21 us: on_device(): w_sum += lax.ppermute(w_sum.astype(BF16), 'xh', SWAP).astype(F32)]
    all_to_all x5 -> x4, waiting for transfers between devices: 21.5 us -> 0.01 us  [the longest x1 0.01 us: on_device(): lax.all_to_all(halves.reshape(NCTX, PIECE, 2 * HALF), ('xl', 'z'), 0, 0,...]
    dot_general x26 -> x0, matrix products: 11 us -> none  [the longest x4 3.64 us: on_device(): jnp.dot(dscore, k_head, preferred_element_type=f32)]
    pallas_call x0 -> x6, Pallas kernels: none -> 8.88 us  [the longest x1 4.98 us: attention_call(): pl.pallas_call(kernel, out_shape=out_shape, in_specs=[SMEM] * 2 + [VMEM]...]
    ppermute x7 -> x13, waiting for transfers between devices: 22.9 us -> 31 us  [the longest x1 14 us: on_device(): from_upper = lax.ppermute(to_lower, 'z', DOWN)]
    all_gather x1 -> x0, waiting for transfers between devices: 6.37 us -> none  [on_device(): w_all = lax.all_gather(w_out, ('xh', 'y', 'c'), axis=0, tiled=True)]
    convert_element_type x9 -> x2, other arithmetic: 6.39 us -> 0.06 us  [the longest x1 0.05 us: on_device(): kv_other.astype(BF16)]
    another operation x9 -> x0, other arithmetic: 3.94 us -> none
  transfers between devices with their start and end apart: 15 -> 19, of which waited for: 6 -> 10; matrix products, arithmetic and copies ran while one was open for 13% -> 2% of each run, Pallas kernels for 0% -> 0%
where the time goes in v2:
time: 164 us; the launch traced here: 162 us
  starting transfers between devices  112 us (68%)
  waiting for transfers between devices  31 us (19%)
  Pallas kernels  8.88 us (5%)
  local copies, waits for them, and re-layouts  4.88 us (3%)
  other arithmetic  3.77 us (2%)
    all_to_all x1, starting transfers between devices, on_device(): lax.all_to_all(halves.reshape(NCTX, PIECE, 2 * HALF), ('xl', 'z'), 0, 0,...  17.1 us
    ppermute x1, waiting for transfers between devices, on_device(): from_upper = lax.ppermute(to_lower, 'z', DOWN)  14 us
    all_to_all x1, starting transfers between devices, on_device(): lax.all_to_all(jnp.concatenate([outgoing, w_sum], 2), ('xl', 'z'), 0, 0,...  12.7 us
    all_to_all x1, starting transfers between devices, on_device(): lax.all_to_all(chosen, 'z', 0, 0, tiled=True).reshape(BLK, NGLOB * 2 * HALF)  11.7 us
    ppermute x1, starting transfers between devices, on_device(): w_sum += lax.ppermute(w_sum.astype(BF16), 'xh', SWAP).astype(F32)  9.21 us
    ppermute x1, starting transfers between devices, on_device(): lax.ppermute(w_core, 'c', SWAP)  8.94 us
    ppermute x1, starting transfers between devices, on_device(): w_sum = w_keep + lax.ppermute(w_send, 'c', SWAP).astype(F32)  7.98 us
    all_to_all x1, starting transfers between devices, on_device(): lax.all_to_all(glob.reshape(NZ, PIECE, NGLOB * 2 * HALF), 'z', 0, 0, tile...  6.51 us
  transfers between devices with their start and end apart: 19, of which 10 were waited for; matrix products, arithmetic and copies ran while one was open for 2% of the time, Pallas kernels for 0%

profile of v2, /device:TPU:1, one launch (start us, length us, event | category | flops | bytes accessed | tf_op | source)
XLA Modules:
  0.0 161.8 jit_solution(9543072739924451700)
XLA Ops:
  0.6 0.9 copy-done.1
  1.5 0.9 copy-done.2
  2.4 0.9 copy-done.3
  3.3 1.2 shard_map.102
  4.6 17.1 %all-to-all-start = ((bf16[32,8,512]{2,1,0:T(8,128)(2,1)}), bf16[32,8,512]{2,1,0:T(8,128)(2,1)S(1)}, u32[]{:S(2)}, u32[]{:S(2)}) async-start(bf16[32,8,512]{2,1,0:T(8,128)(2,1)} %bitcast.3), calls=%async_computation | async-start | bytes 524288 | tf_op jit(solution)/shard_map/all_to_all | solution.py:234
  21.7 3.1 %collective-permute-start = (bf16[128,768]{1,0:T(8,128)(2,1)S(1)}, bf16[128,768]{1,0:T(8,128)(2,1)S(1)}, u32[]{:S(2)}, u32[]{:S(2)}) collective-permute-start(bf16[128,768]{1,0:T(8,128)(2,1)S(1)} %get-tuple-element.20), channel_id=1, source_target_pairs={{0,16},{16,0},{1,17},{17,1},{2,18},{18,2},{3,19},{19,3},{4,20},{20... | collective-permute-start | bytes 589832 | tf_op jit(solution)/shard_map/ppermute | solution.py:237
  24.9 2.1 %collective-permute-start.5 = (bf16[128,1024]{1,0:T(8,128)(2,1)S(1)}, bf16[128,1024]{1,0:T(8,128)(2,1)S(1)}, u32[]{:S(2)}, u32[]{:S(2)}) collective-permute-start(bf16[128,1024]{1,0:T(8,128)(2,1)S(1)} %bitcast.36), channel_id=1, source_target_pairs={{0,16},{16,0},{1,17},{17,1},{2,18},{18,2},{3,19},{19,3},{4,20},{20... | collective-permute-start | bytes 786440 | tf_op jit(solution)/shard_map/ppermute | solution.py:243
  27.0 2.6 %collective-permute-done.other_ref.refs_3_ = bf16[128,768]{1,0:T(8,128)(2,1)S(1)} collective-permute-done((bf16[128,768]{1,0:T(8,128)(2,1)S(1)}, bf16[128,768]{1,0:T(8,128)(2,1)S(1)}, u32[]{:S(2)}, u32[]{:S(2)}) %collective-permute-start) | collective-permute-done | bytes 196640 | tf_op jit(solution)/shard_map/ppermute | solution.py:237
  29.6 3.1 %collective-permute-start.1 = (bf16[2,128,512]{2,1,0:T(8,128)(2,1)S(1)}, bf16[2,128,512]{2,1,0:T(8,128)(2,1)S(1)}, u32[]{:S(2)}, u32[]{:S(2)}) collective-permute-start(bf16[2,128,512]{2,1,0:T(8,128)(2,1)S(1)} %shard_map.103), channel_id=1, source_target_pairs={{0,1},{1,2},{2,3},{3,4},{4,5},{5,6},{6,7},{7,8},{8,9},{9,10},{10,1... | collective-permute-start | bytes 786440 | tf_op jit(solution)/shard_map/ppermute | solution.py:240
  32.7 3.6 %collective-permute-start.2 = (bf16[2,128,512]{2,1,0:T(8,128)(2,1)S(1)}, bf16[2,128,512]{2,1,0:T(8,128)(2,1)S(1)}, u32[]{:S(2)}, u32[]{:S(2)}) collective-permute-start(bf16[2,128,512]{2,1,0:T(8,128)(2,1)S(1)} %shard_map.103), channel_id=1, source_target_pairs={{0,15},{1,0},{2,1},{3,2},{4,3},{5,4},{6,5},{7,6},{8,7},{9,8},{10,9... | collective-permute-start | bytes 786440 | tf_op jit(solution)/shard_map/ppermute | solution.py:241
  36.3 0.7 collective-permute-start.3
  36.9 3.2 %collective-permute-start.4 = (bf16[32,1024]{1,0:T(8,128)(2,1)S(1)}, bf16[32,1024]{1,0:T(8,128)(2,1)S(1)}, u32[]{:S(2)}, u32[]{:S(2)}) collective-permute-start(bf16[32,1024]{1,0:T(8,128)(2,1)S(1)} %collective-permute-done.3), channel_id=1, source_target_pairs={{0,64},{64,0},{128,192},{192,128},{1,65},{65,1},{129,193},{193,129... | collective-permute-start | bytes 196616 | tf_op jit(solution)/shard_map/ppermute | solution.py:242
  40.2 2.1 %collective-permute-done.4.refs_2_ = bf16[32,1024]{1,0:T(8,128)(2,1)S(1)} collective-permute-done((bf16[32,1024]{1,0:T(8,128)(2,1)S(1)}, bf16[32,1024]{1,0:T(8,128)(2,1)S(1)}, u32[]{:S(2)}, u32[]{:S(2)}) %collective-permute-start.4) | collective-permute-done | bytes 65568 | tf_op jit(solution)/shard_map/ppermute | solution.py:242
  42.3 1.3 shard_map.104
  43.6 11.7 %all-to-all-start.1 = ((bf16[16,8,1536]{2,1,0:T(8,128)(2,1)}), bf16[16,8,1536]{2,1,0:T(8,128)(2,1)S(1)}, u32[]{:S(2)}, u32[]{:S(2)}) async-start(bf16[16,8,1536]{2,1,0:T(8,128)(2,1)} %shard_map.104), calls=%async_computation.1 | async-start | bytes 786432 | tf_op jit(solution)/shard_map/all_to_all | solution.py:250
  55.3 4.8 %collective-permute-start.6 = (bf16[64,1024]{1,0:T(8,128)(2,1)S(1)}, bf16[64,1024]{1,0:T(8,128)(2,1)S(1)}, u32[]{:S(2)}, u32[]{:S(2)}) collective-permute-start(bf16[64,1024]{1,0:T(8,128)(2,1)S(1)} %pad_maximum_fusion.2), channel_id=1, source_target_pairs={{0,128},{64,192},{128,0},{192,64},{1,129},{65,193},{129,1},{193,65... | collective-permute-start | bytes 393224 | tf_op jit(solution)/shard_map/ppermute | solution.py:252
  60.2 2.3 %collective-permute-done.6 = bf16[64,1024]{1,0:T(8,128)(2,1)S(1)} collective-permute-done((bf16[64,1024]{1,0:T(8,128)(2,1)S(1)}, bf16[64,1024]{1,0:T(8,128)(2,1)S(1)}, u32[]{:S(2)}, u32[]{:S(2)}) %collective-permute-start.6) | collective-permute-done | bytes 131104 | tf_op jit(solution)/shard_map/ppermute | solution.py:252
  62.5 8.9 %collective-permute-start.7 = (bf16[128,1024]{1,0:T(8,128)(2,1)S(1)}, bf16[128,1024]{1,0:T(8,128)(2,1)S(1)}, u32[]{:S(2)}, u32[]{:S(2)}) collective-permute-start(bf16[128,1024]{1,0:T(8,128)(2,1)S(1)} %constant_dynamic-update-slice_fusion.w_ref), channel_id=1, source_target_pairs={{0,32},{32,0},{1,33},{33,1},{2,34},{34,2},{3,35},{35,3},{4,36},{36... | collective-permute-start | bytes 786440 | tf_op jit(solution)/shard_map/ppermute | solution.py:256
  71.5 0.1 copy.11.refs_0_
  71.6 1.0 collective-permute-done.7.w_other_ref
  72.6 0.5 shard_map.105
  73.1 5.0 %shard_map.106 = (bf16[2,128,256]{2,1,0:T(8,128)(2,1)S(1)}, f32[2,128,512]{2,1,0:T(8,128)S(1)}, bf16[2,128,512]{2,1,0:T(8,128)(2,1)S(1)}, bf16[2,128,512]{2,1,0:...) custom-call(s32[32,3]{1,0:T(8,128)S(1)} %copy.11.refs_0_, ...), custom_call_target="tpu_custom_call" | custom-call | flops 1000000000 | bytes 5242880 | tf_op jit(solution)/shard_map/pallas_call | solution.py:192
  78.1 0.7 copy-done.5
  78.8 0.7 copy-done.7
  79.5 8.0 %collective-permute-start.11 = (bf16[4,32,1024]{2,1,0:T(8,128)(2,1)S(1)}, bf16[4,32,1024]{2,1,0:T(8,128)(2,1)S(1)}, u32[]{:S(2)}, u32[]{:S(2)}) collective-permute-start(bf16[4,32,1024]{2,1,0:T(8,128)(2,1)S(1)} %get-tuple-element.30), channel_id=1, source_target_pairs={{0,32},{32,0},{1,33},{33,1},{2,34},{34,2},{3,35},{35,3},{4,36},{36... | collective-permute-start | bytes 786440 | tf_op jit(solution)/shard_map/ppermute | solution.py:269
  87.5 6.5 %all-to-all-start.2 = ((bf16[16,8,1536]{2,1,0:T(8,128)(2,1)}), bf16[16,8,1536]{2,1,0:T(8,128)(2,1)S(1)}, u32[]{:S(2)}, u32[]{:S(2)}) async-start(bf16[16,8,1536]{2,1,0:T(8,128)(2,1)} %bitcast.9), calls=%async_computation.2 | async-start | bytes 786432 | tf_op jit(solution)/shard_map/all_to_all | solution.py:266
  94.0 0.1 convert_add_fusion
  94.1 4.8 %collective-permute-start.12 = (bf16[2,32,1024]{2,1,0:T(8,128)(2,1)S(1)}, bf16[2,32,1024]{2,1,0:T(8,128)(2,1)S(1)}, u32[]{:S(2)}, u32[]{:S(2)}) collective-permute-start(bf16[2,32,1024]{2,1,0:T(8,128)(2,1)S(1)} %slice.93), channel_id=1, source_target_pairs={{0,128},{64,192},{128,0},{192,64},{1,129},{65,193},{129,1},{193,65... | collective-permute-start | bytes 393224 | tf_op jit(solution)/shard_map/ppermute | solution.py:270
  99.0 0.6 fusion.6
  99.5 2.8 %collective-permute-done.12 = bf16[2,32,1024]{2,1,0:T(8,128)(2,1)S(1)} collective-permute-done((bf16[2,32,1024]{2,1,0:T(8,128)(2,1)S(1)}, bf16[2,32,1024]{2,1,0:T(8,128)(2,1)S(1)}, u32[]{:S(2)}, u32[]{:S(2)}) %collective-permute-start.12) | collective-permute-done | bytes 131104 | tf_op jit(solution)/shard_map/ppermute | solution.py:270
  102.4 3.2 %collective-permute-start.13 = (bf16[32,1024]{1,0:T(8,128)(2,1)S(1)}, bf16[32,1024]{1,0:T(8,128)(2,1)S(1)}, u32[]{:S(2)}, u32[]{:S(2)}) collective-permute-start(bf16[32,1024]{1,0:T(8,128)(2,1)S(1)} %fusion.4), channel_id=1, source_target_pairs={{0,64},{64,0},{128,192},{192,128},{1,65},{65,1},{129,193},{193,129... | collective-permute-start | bytes 196616 | tf_op jit(solution)/shard_map/ppermute | solution.py:271
  105.6 1.3 iota_compare_fusion
  106.9 0.8 collective-permute-done.13
  107.7 9.2 %collective-permute-start.14 = (bf16[32,1024]{1,0:T(8,128)(2,1)S(1)}, bf16[32,1024]{1,0:T(8,128)(2,1)S(1)}, u32[]{:S(2)}, u32[]{:S(2)}) collective-permute-start(bf16[32,1024]{1,0:T(8,128)(2,1)S(1)} %fusion.2), channel_id=1, source_target_pairs={{0,256},{256,0},{1,257},{257,1},{2,258},{258,2},{3,259},{259,3},{4... | collective-permute-start | bytes 196616 | tf_op jit(solution)/shard_map/ppermute | solution.py:272
  116.9 0.7 iota_compare_fusion.2
  117.6 1.3 collective-permute-done.14
  118.9 0.1 reduce_sum.21
  119.0 0.2 select_select_fusion
  119.2 0.8 pad_maximum_fusion
  119.9 12.7 %all-to-all-start.3 = ((bf16[32,8,640]{2,1,0:T(8,128)(2,1)}), bf16[32,8,640]{2,1,0:T(8,128)(2,1)S(1)}, u32[]{:S(2)}, u32[]{:S(2)}) async-start(bf16[32,8,640]{2,1,0:T(8,128)(2,1)} %pad_maximum_fusion), calls=%async_computation.3 | async-start | bytes 655360 | tf_op jit(solution)/shard_map/all_to_all | solution.py:287
  132.7 4.4 %collective-permute-start.8 = (bf16[2,128,512]{2,1,0:T(8,128)(2,1)S(1)}, bf16[2,128,512]{2,1,0:T(8,128)(2,1)S(1)}, u32[]{:S(2)}, u32[]{:S(2)}) collective-permute-start(bf16[2,128,512]{2,1,0:T(8,128)(2,1)S(1)} %copy-done.8), channel_id=1, source_target_pairs={{0,15},{1,0},{2,1},{3,2},{4,3},{5,4},{6,5},{7,6},{8,7},{9,8},{10,9... | collective-permute-start | bytes 786440 | tf_op jit(solution)/shard_map/ppermute | solution.py:276
  137.1 1.9 %collective-permute-start.9 = (bf16[2,128,512]{2,1,0:T(8,128)(2,1)S(1)}, bf16[2,128,512]{2,1,0:T(8,128)(2,1)S(1)}, u32[]{:S(2)}, u32[]{:S(2)}) collective-permute-start(bf16[2,128,512]{2,1,0:T(8,128)(2,1)S(1)} %copy-done.6), channel_id=1, source_target_pairs={{0,1},{1,2},{2,3},{3,4},{4,5},{5,6},{6,7},{7,8},{8,9},{9,10},{10,1... | collective-permute-start | bytes 786440 | tf_op jit(solution)/shard_map/ppermute | solution.py:277
  139.0 14.0 %collective-permute-done.8.upper_ref = bf16[2,128,512]{2,1,0:T(8,128)(2,1)S(1)} collective-permute-done((bf16[2,128,512]{2,1,0:T(8,128)(2,1)S(1)}, bf16[2,128,512]{2,1,0:T(8,128)(2,1)S(1)}, u32[]{:S(2)}, u32[]{:S(2)}) %collective-permute-start.8) | collective-permute-done | bytes 262176 | tf_op jit(solution)/shard_map/ppermute | solution.py:276
  153.0 1.6 collective-permute-done.9.lower_ref
  154.6 3.2 %collective-permute-start.10 = (bf16[128,768]{1,0:T(8,128)(2,1)S(1)}, bf16[128,768]{1,0:T(8,128)(2,1)S(1)}, u32[]{:S(2)}, u32[]{:S(2)}) collective-permute-start(bf16[128,768]{1,0:T(8,128)(2,1)S(1)} %pad_maximum_fusion.1), channel_id=1, source_target_pairs={{0,16},{16,0},{1,17},{17,1},{2,18},{18,2},{3,19},{19,3},{4,20},{20... | collective-permute-start | bytes 589832 | tf_op jit(solution)/shard_map/ppermute | solution.py:279
  157.9 0.6 convert_reduce_fusion
  158.5 2.5 %collective-permute-done.10.back_ref = bf16[128,768]{1,0:T(8,128)(2,1)S(1)} collective-permute-done((bf16[128,768]{1,0:T(8,128)(2,1)S(1)}, bf16[128,768]{1,0:T(8,128)(2,1)S(1)}, u32[]{:S(2)}, u32[]{:S(2)}) %collective-permute-start.10) | collective-permute-done | bytes 196640 | tf_op jit(solution)/shard_map/ppermute | solution.py:279
  161.0 0.8 shard_map.107
  (41 shorter events, 0.3 us)
Async XLA Ops:
  0.6 0.9 copy-start.1
  1.5 0.9 copy-start.2
  2.4 0.9 copy-start.3
  4.6 20.3 %copy-start = (bf16[1,128,1024]{2,1,0:T(8,128)(2,1)S(1)}, bf16[1,128,1024]{2,1,0:T(8,128)(2,1)}, u32[]{:S(2)}) copy-start(bf16[1,128,1024]{2,1,0:T(8,128)(2,1)} %param.10) | copy-start | bytes 786436
  4.6 37.7 %all-to-all-start = ((bf16[32,8,512]{2,1,0:T(8,128)(2,1)}), bf16[32,8,512]{2,1,0:T(8,128)(2,1)S(1)}, u32[]{:S(2)}, u32[]{:S(2)}) async-start(bf16[32,8,512]{2,1,0:T(8,128)(2,1)} %bitcast.3), calls=%async_computation | async-start | bytes 524288 | tf_op jit(solution)/shard_map/all_to_all | solution.py:234
  21.7 7.9 %collective-permute-start = (bf16[128,768]{1,0:T(8,128)(2,1)S(1)}, bf16[128,768]{1,0:T(8,128)(2,1)S(1)}, u32[]{:S(2)}, u32[]{:S(2)}) collective-permute-start(bf16[128,768]{1,0:T(8,128)(2,1)S(1)} %get-tuple-element.20), channel_id=1, source_target_pairs={{0,16},{16,0},{1,17},{17,1},{2,18},{18,2},{3,19},{19,3},{4,20},{20... | collective-permute-start | bytes 589832 | tf_op jit(solution)/shard_map/ppermute | solution.py:237
  24.9 17.4 %collective-permute-start.5 = (bf16[128,1024]{1,0:T(8,128)(2,1)S(1)}, bf16[128,1024]{1,0:T(8,128)(2,1)S(1)}, u32[]{:S(2)}, u32[]{:S(2)}) collective-permute-start(bf16[128,1024]{1,0:T(8,128)(2,1)S(1)} %bitcast.36), channel_id=1, source_target_pairs={{0,16},{16,0},{1,17},{17,1},{2,18},{18,2},{3,19},{19,3},{4,20},{20... | collective-permute-start | bytes 786440 | tf_op jit(solution)/shard_map/ppermute | solution.py:243
  29.6 6.7 %copy-start.10 = (bf16[32,1024]{1,0:T(8,128)(2,1)S(1)}, bf16[32,1024]{1,0:T(8,128)(2,1)}, u32[]{:S(2)}) copy-start(bf16[32,1024]{1,0:T(8,128)(2,1)} %param.11) | copy-start | bytes 196612
  29.6 12.7 %copy-start.4 = (s32[3]{0:T(128)S(1)}, s32[3]{0:T(128)}, u32[]{:S(2)}) copy-start(s32[3]{0:T(128)} %refs_1_.1) | copy-start | bytes 40
  29.6 12.6 %collective-permute-start.1 = (bf16[2,128,512]{2,1,0:T(8,128)(2,1)S(1)}, bf16[2,128,512]{2,1,0:T(8,128)(2,1)S(1)}, u32[]{:S(2)}, u32[]{:S(2)}) collective-permute-start(bf16[2,128,512]{2,1,0:T(8,128)(2,1)S(1)} %shard_map.103), channel_id=1, source_target_pairs={{0,1},{1,2},{2,3},{3,4},{4,5},{5,6},{6,7},{7,8},{8,9},{9,10},{10,1... | collective-permute-start | bytes 786440 | tf_op jit(solution)/shard_map/ppermute | solution.py:240
  32.7 9.6 %collective-permute-start.2 = (bf16[2,128,512]{2,1,0:T(8,128)(2,1)S(1)}, bf16[2,128,512]{2,1,0:T(8,128)(2,1)S(1)}, u32[]{:S(2)}, u32[]{:S(2)}) collective-permute-start(bf16[2,128,512]{2,1,0:T(8,128)(2,1)S(1)} %shard_map.103), channel_id=1, source_target_pairs={{0,15},{1,0},{2,1},{3,2},{4,3},{5,4},{6,5},{7,6},{8,7},{9,8},{10,9... | collective-permute-start | bytes 786440 | tf_op jit(solution)/shard_map/ppermute | solution.py:241
  36.3 0.7 collective-permute-start.3
  36.9 5.3 %collective-permute-start.4 = (bf16[32,1024]{1,0:T(8,128)(2,1)S(1)}, bf16[32,1024]{1,0:T(8,128)(2,1)S(1)}, u32[]{:S(2)}, u32[]{:S(2)}) collective-permute-start(bf16[32,1024]{1,0:T(8,128)(2,1)S(1)} %collective-permute-done.3), channel_id=1, source_target_pairs={{0,64},{64,0},{128,192},{192,128},{1,65},{65,1},{129,193},{193,129... | collective-permute-start | bytes 196616 | tf_op jit(solution)/shard_map/ppermute | solution.py:242
  43.6 29.5 %all-to-all-start.1 = ((bf16[16,8,1536]{2,1,0:T(8,128)(2,1)}), bf16[16,8,1536]{2,1,0:T(8,128)(2,1)S(1)}, u32[]{:S(2)}, u32[]{:S(2)}) async-start(bf16[16,8,1536]{2,1,0:T(8,128)(2,1)} %shard_map.104), calls=%async_computation.1 | async-start | bytes 786432 | tf_op jit(solution)/shard_map/all_to_all | solution.py:250
  55.3 7.2 %collective-permute-start.6 = (bf16[64,1024]{1,0:T(8,128)(2,1)S(1)}, bf16[64,1024]{1,0:T(8,128)(2,1)S(1)}, u32[]{:S(2)}, u32[]{:S(2)}) collective-permute-start(bf16[64,1024]{1,0:T(8,128)(2,1)S(1)} %pad_maximum_fusion.2), channel_id=1, source_target_pairs={{0,128},{64,192},{128,0},{192,64},{1,129},{65,193},{129,1},{193,65... | collective-permute-start | bytes 393224 | tf_op jit(solution)/shard_map/ppermute | solution.py:252
  60.1 11.3 %copy-start.9 = (s32[32,3]{0,1:T(4,128)S(1)}, s32[32,3]{0,1:T(4,128)}, u32[]{:S(2)}) copy-start(s32[32,3]{0,1:T(4,128)} %param.12) | copy-start | bytes 1156
  62.5 10.1 %collective-permute-start.7 = (bf16[128,1024]{1,0:T(8,128)(2,1)S(1)}, bf16[128,1024]{1,0:T(8,128)(2,1)S(1)}, u32[]{:S(2)}, u32[]{:S(2)}) collective-permute-start(bf16[128,1024]{1,0:T(8,128)(2,1)S(1)} %constant_dynamic-update-slice_fusion.w_ref), channel_id=1, source_target_pairs={{0,32},{32,0},{1,33},{33,1},{2,34},{34,2},{3,35},{35,3},{4,36},{36... | collective-permute-start | bytes 786440 | tf_op jit(solution)/shard_map/ppermute | solution.py:256
  78.1 0.7 copy-start.5
  78.8 0.7 copy-start.7
  79.5 14.5 %collective-permute-start.11 = (bf16[4,32,1024]{2,1,0:T(8,128)(2,1)S(1)}, bf16[4,32,1024]{2,1,0:T(8,128)(2,1)S(1)}, u32[]{:S(2)}, u32[]{:S(2)}) collective-permute-start(bf16[4,32,1024]{2,1,0:T(8,128)(2,1)S(1)} %get-tuple-element.30), channel_id=1, source_target_pairs={{0,32},{32,0},{1,33},{33,1},{2,34},{34,2},{3,35},{35,3},{4,36},{36... | collective-permute-start | bytes 786440 | tf_op jit(solution)/shard_map/ppermute | solution.py:269
  87.5 31.4 %all-to-all-start.2 = ((bf16[16,8,1536]{2,1,0:T(8,128)(2,1)}), bf16[16,8,1536]{2,1,0:T(8,128)(2,1)S(1)}, u32[]{:S(2)}, u32[]{:S(2)}) async-start(bf16[16,8,1536]{2,1,0:T(8,128)(2,1)} %bitcast.9), calls=%async_computation.2 | async-start | bytes 786432 | tf_op jit(solution)/shard_map/all_to_all | solution.py:266
  94.1 8.2 %collective-permute-start.12 = (bf16[2,32,1024]{2,1,0:T(8,128)(2,1)S(1)}, bf16[2,32,1024]{2,1,0:T(8,128)(2,1)S(1)}, u32[]{:S(2)}, u32[]{:S(2)}) collective-permute-start(bf16[2,32,1024]{2,1,0:T(8,128)(2,1)S(1)} %slice.93), channel_id=1, source_target_pairs={{0,128},{64,192},{128,0},{192,64},{1,129},{65,193},{129,1},{193,65... | collective-permute-start | bytes 393224 | tf_op jit(solution)/shard_map/ppermute | solution.py:270
  102.4 5.3 %collective-permute-start.13 = (bf16[32,1024]{1,0:T(8,128)(2,1)S(1)}, bf16[32,1024]{1,0:T(8,128)(2,1)S(1)}, u32[]{:S(2)}, u32[]{:S(2)}) collective-permute-start(bf16[32,1024]{1,0:T(8,128)(2,1)S(1)} %fusion.4), channel_id=1, source_target_pairs={{0,64},{64,0},{128,192},{192,128},{1,65},{65,1},{129,193},{193,129... | collective-permute-start | bytes 196616 | tf_op jit(solution)/shard_map/ppermute | solution.py:271
  107.7 11.2 %collective-permute-start.14 = (bf16[32,1024]{1,0:T(8,128)(2,1)S(1)}, bf16[32,1024]{1,0:T(8,128)(2,1)S(1)}, u32[]{:S(2)}, u32[]{:S(2)}) collective-permute-start(bf16[32,1024]{1,0:T(8,128)(2,1)S(1)} %fusion.2), channel_id=1, source_target_pairs={{0,256},{256,0},{1,257},{257,1},{2,258},{258,2},{3,259},{259,3},{4... | collective-permute-start | bytes 196616 | tf_op jit(solution)/shard_map/ppermute | solution.py:272
  119.9 12.8 %copy-start.8 = (bf16[2,128,512]{2,1,0:T(8,128)(2,1)S(1)}, bf16[2,128,512]{2,1,0:T(8,128)(2,1)}, u32[]{:S(2)}) copy-start(bf16[2,128,512]{2,1,0:T(8,128)(2,1)} %copy-done.7) | copy-start | bytes 786436
  119.9 17.1 %copy-start.6 = (bf16[2,128,512]{2,1,0:T(8,128)(2,1)S(1)}, bf16[2,128,512]{2,1,0:T(8,128)(2,1)}, u32[]{:S(2)}) copy-start(bf16[2,128,512]{2,1,0:T(8,128)(2,1)} %copy-done.5) | copy-start | bytes 786436
  119.9 37.9 %all-to-all-start.3 = ((bf16[32,8,640]{2,1,0:T(8,128)(2,1)}), bf16[32,8,640]{2,1,0:T(8,128)(2,1)S(1)}, u32[]{:S(2)}, u32[]{:S(2)}) async-start(bf16[32,8,640]{2,1,0:T(8,128)(2,1)} %pad_maximum_fusion), calls=%async_computation.3 | async-start | bytes 655360 | tf_op jit(solution)/shard_map/all_to_all | solution.py:287
  132.7 20.3 %collective-permute-start.8 = (bf16[2,128,512]{2,1,0:T(8,128)(2,1)S(1)}, bf16[2,128,512]{2,1,0:T(8,128)(2,1)S(1)}, u32[]{:S(2)}, u32[]{:S(2)}) collective-permute-start(bf16[2,128,512]{2,1,0:T(8,128)(2,1)S(1)} %copy-done.8), channel_id=1, source_target_pairs={{0,15},{1,0},{2,1},{3,2},{4,3},{5,4},{6,5},{7,6},{8,7},{9,8},{10,9... | collective-permute-start | bytes 786440 | tf_op jit(solution)/shard_map/ppermute | solution.py:276
  137.1 17.5 %collective-permute-start.9 = (bf16[2,128,512]{2,1,0:T(8,128)(2,1)S(1)}, bf16[2,128,512]{2,1,0:T(8,128)(2,1)S(1)}, u32[]{:S(2)}, u32[]{:S(2)}) collective-permute-start(bf16[2,128,512]{2,1,0:T(8,128)(2,1)S(1)} %copy-done.6), channel_id=1, source_target_pairs={{0,1},{1,2},{2,3},{3,4},{4,5},{5,6},{6,7},{7,8},{8,9},{9,10},{10,1... | collective-permute-start | bytes 786440 | tf_op jit(solution)/shard_map/ppermute | solution.py:277
  154.6 6.4 %collective-permute-start.10 = (bf16[128,768]{1,0:T(8,128)(2,1)S(1)}, bf16[128,768]{1,0:T(8,128)(2,1)S(1)}, u32[]{:S(2)}, u32[]{:S(2)}) collective-permute-start(bf16[128,768]{1,0:T(8,128)(2,1)S(1)} %pad_maximum_fusion.1), channel_id=1, source_target_pairs={{0,16},{16,0},{1,17},{17,1},{2,18},{18,2},{3,19},{19,3},{4,20},{20... | collective-permute-start | bytes 589832 | tf_op jit(solution)/shard_map/ppermute | solution.py:279

commit v3 on v2

--- a/solution.py
+++ b/solution.py
@@ -19,13 +19,16 @@
 UP = [(i, (i + 1) % NZ) for i in range(NZ)]
 DOWN = [(i, (i - 1) % NZ) for i in range(NZ)]
 SWAP = [(0, 1), (1, 0)]
+
 CROSS = [(0, 0), (1, 2), (2, 1), (3, 3)]
+
 Y_ONE = [(i, i ^ 1) for i in range(NY)]
 Y_TWO = [(i, i ^ 2) for i in range(NY)]
 
 VMEM = pl.BlockSpec(memory_space=pltpu.VMEM)
 SMEM = pl.BlockSpec(memory_space=pltpu.SMEM)
 ANY = pl.BlockSpec(memory_space=pl.ANY)
+HBM = pl.BlockSpec(memory_space=pltpu.HBM)
 BF16, F32 = jnp.bfloat16, jnp.float32
 
 
@@ -33,14 +36,14 @@
     return jax.ShapeDtypeStruct(shape, dtype)
 
 
-def call(kernel, specs, operands, out_shape, scratch=(), flops=0, nbytes=2**20):
+def call(kernel, specs, operands, out_shape, scratch=(), flops=0, nbytes=2**20, vmem=8):
     return pl.pallas_call(
         kernel,
         out_shape=out_shape,
         in_specs=specs,
         out_specs=jax.tree.map(lambda _: VMEM, out_shape),
         scratch_shapes=scratch,
-        compiler_params=pltpu.CompilerParams(vmem_limit_bytes=32 * 2**20),
+        compiler_params=pltpu.CompilerParams(vmem_limit_bytes=vmem * 2**20),
         cost_estimate=pl.CostEstimate(flops=flops, bytes_accessed=nbytes, transcendentals=0),
     )(*operands)
 
@@ -79,6 +82,24 @@
         send_ref[:, lanes] = jnp.where(first, high, low)
 
 
+def is_global(globals_ref, block):
+    found = block == globals_ref[0]
+    for g in range(1, NGLOB):
+        found = found | (block == globals_ref[g])
+    return found
+
+
+def place(globals_ref, g):
+    block = globals_ref[g]
+    second = (block >= NZ) & is_global(globals_ref, block - NZ)
+    return jnp.where(block >= NZ, block - NZ, block), second
+
+
+def first_slot(globals_ref):
+    lower_slot = lax.axis_index("xl")
+    return jnp.where(is_global(globals_ref, lax.axis_index("z")), lower_slot, 1 - lower_slot)
+
+
 def stack_kernel(mine_ref, other_ref, kv_ref):
     kv_ref[0] = mine_ref[:, : 2 * HALF]
     kv_ref[1] = other_ref[:, : 2 * HALF]
@@ -92,7 +113,7 @@
             chosen_ref[z, :, g * 2 * HALF : (g + 1) * 2 * HALF] = piece
 
 
-def project_kernel(w_ref, w_other_ref, grad_ref, grad_other_ref, d_ref, d_other_ref, w_scr):
+def project_kernel(grad_ref, grad_other_ref, w_ref, w_other_ref, d_ref, d_other_ref, w_scr):
     for j, ref in enumerate((w_ref, w_other_ref)):
         for i in range(NY):
             w_scr[shard_rows(i, j)] = ref[i * NCTX : (i + 1) * NCTX]
@@ -199,61 +220,106 @@
             pltpu.VMEM((2 * BLK, HALF), BF16),
             pltpu.VMEM((HALF, DM), F32),
         ],
-        compiler_params=pltpu.CompilerParams(vmem_limit_bytes=32 * 2**20),
+        compiler_params=pltpu.CompilerParams(vmem_limit_bytes=24 * 2**20),
         cost_estimate=pl.CostEstimate(
             flops=10**9, bytes_accessed=5 * 2**20, transcendentals=400000
         ),
     )(*operands)
 
 
-def final_kernel(dq_ref, own_ref, upper_ref, lower_ref, back_ref, owned_ref, q_ref, k_ref, v_ref):
+def outgoing_kernel(globals_ref, glob_ref, w_ref, out_ref, second_ref):
+    total = glob_ref[0].astype(F32)
+    for z in range(1, NZ):
+        total += glob_ref[z].astype(F32)
+    out_ref[:, :, : 2 * HALF] = jnp.zeros((NZ, PIECE, 2 * HALF), BF16)
+    out_ref[:, :, 2 * HALF :] = w_ref[...]
+    second_ref[...] = jnp.zeros((NZ, PIECE, 2 * HALF), BF16)
+    for g in range(NGLOB):
+        part = total[:, g * 2 * HALF : (g + 1) * 2 * HALF].astype(BF16)
+        column, second = place(globals_ref, g)
+
+        @pl.when(second)
+        def _():
+            second_ref[column] = part
+
+        @pl.when(jnp.logical_not(second))
+        def _():
+            out_ref[column, :, : 2 * HALF] = part
+
+
+def combine_kernel(
+    globals_ref, dq_ref, own_ref, upper_ref, lower_ref, owned_ref, second_ref, kv_ref, back_ref
+):
+    first = first_slot(globals_ref)
+    upper_slot = 1 - lax.axis_index("xl")
+    owned = owned_ref[:, : 2 * HALF].astype(F32)
+    second = second_ref[...].astype(F32)
+    for slot in range(2):
+        total = own_ref[slot] + upper_ref[slot].astype(F32) + lower_ref[slot].astype(F32)
+        total += jnp.where(first == slot, owned, 0.0)
+        total += jnp.where(upper_slot == slot, second, 0.0)
+        if slot == 0:
+            kv_ref[...] = total.astype(BF16)
+        else:
+            back_ref[:, HALF:] = total.astype(BF16)
+            back_ref[:, :HALF] = dq_ref[1]
+
+
+def final_kernel(dq_ref, kv_ref, back_ref, q_ref, k_ref, v_ref):
     first = lax.axis_index("xl") == 0
-    own = own_ref[0] + upper_ref[0].astype(F32) + lower_ref[0].astype(F32)
     for half in range(2):
         mine = first if half == 0 else jnp.logical_not(first)
-        back = back_ref[:, HALF:].astype(F32)
-        owned = owned_ref[half * BLK : (half + 1) * BLK, : 2 * HALF].astype(F32)
-        kv = (jnp.where(mine, own, back) + owned).astype(BF16)
         lanes = slice(half * HALF, (half + 1) * HALF)
-        k_ref[:, lanes] = kv[:, :HALF]
-        v_ref[:, lanes] = kv[:, HALF:]
         q_ref[:, lanes] = jnp.where(mine, dq_ref[0], back_ref[:, :HALF])
+        k_ref[:, lanes] = jnp.where(mine, kv_ref[:, :HALF], back_ref[:, HALF : 2 * HALF])
+        v_ref[:, lanes] = jnp.where(mine, kv_ref[:, HALF:], back_ref[:, 2 * HALF :])
+
+
+def over_columns(array):
+    return lax.all_to_all(array.reshape(NZ, PIECE, -1), "z", 0, 0, tiled=True)
 
 
 def on_device(query, key, value, out_grad, w_out, band_tiles, global_blocks):
     xl = lax.axis_index("xl")
     q, k, v, grad = query[0], key[0], value[0], out_grad[0]
 
+    folded = global_blocks % NZ
+    clash = (
+        (folded[0] == folded[1]) | (folded[0] == folded[2]) | (folded[1] == folded[2])
+    )
+    nothing = jnp.zeros((NZ, PIECE, 2 * HALF), BF16)
+
     halves, mine, send = call(
         split_kernel,
-        [ANY] * 3,
+        [HBM] * 3,
         (q, k, v),
         (shaped((2, BLK, 2 * HALF)), shaped((BLK, 3 * HALF)), shaped((BLK, 3 * HALF))),
         [pltpu.VMEM((3, BLK, 2 * HALF), BF16), pltpu.SemaphoreType.DMA((3,))],
+        vmem=56,
     )
     pieces = lax.all_to_all(
         halves.reshape(NCTX, PIECE, 2 * HALF), ("xl", "z"), 0, 0, tiled=True
     )
     other = lax.ppermute(send, "xl", SWAP)
+    grad_other = lax.ppermute(grad, "xl", SWAP)
     w0 = lax.ppermute(w_out, ("xh", "xl"), CROSS)
+    w1 = lax.ppermute(w0, "y", Y_ONE)
     kv = call(stack_kernel, [VMEM] * 2, (mine, other), shaped((2, BLK, 2 * HALF)))
     before = lax.ppermute(kv, "z", UP)
     after = lax.ppermute(kv, "z", DOWN)
-    w1 = lax.ppermute(w0, "y", Y_ONE)
-    grad_other = lax.ppermute(grad, "xl", SWAP)
     chosen = call(
         choose_kernel,
         [SMEM, VMEM] + [ANY] * 4,
         (global_blocks, pieces, before, after, w1, grad_other),
         shaped((NZ, PIECE, NGLOB * 2 * HALF)),
     )
-    shared = lax.all_to_all(chosen, "z", 0, 0, tiled=True).reshape(BLK, NGLOB * 2 * HALF)
+    shared = over_columns(chosen).reshape(BLK, NGLOB * 2 * HALF)
     w01 = jnp.concatenate([w0, w1], 0)
     w_core = jnp.concatenate([w01, lax.ppermute(w01, "y", Y_TWO)], 0)
     d_mine, d_other = call(
         project_kernel,
         [VMEM] * 4,
-        (w_core, lax.ppermute(w_core, "c", SWAP), grad, grad_other),
+        (grad, grad_other, w_core, lax.ppermute(w_core, "c", SWAP)),
         (shaped((BLK, HALF)), shaped((BLK, HALF))),
         [pltpu.VMEM((HALF, DM), BF16)],
     )
@@ -263,36 +329,40 @@
         d_mine, d_other, grad, grad_other,
     )
 
-    glob = lax.all_to_all(
-        glob.reshape(NZ, PIECE, NGLOB * 2 * HALF), "z", 0, 0, tiled=True
-    )
+    glob = over_columns(glob)
     w_sum = w_keep + lax.ppermute(w_send, "c", SWAP).astype(F32)
     w_sum = w_sum[:2] + lax.ppermute(w_sum[2:].astype(BF16), "y", Y_TWO).astype(F32)
     w_sum = w_sum[0] + lax.ppermute(w_sum[1].astype(BF16), "y", Y_ONE).astype(F32)
-    w_sum += lax.ppermute(w_sum.astype(BF16), "xh", SWAP).astype(F32)
-    w_sum = jnp.where(lax.axis_index("xh") == xl, w_sum, 0.0).astype(BF16)
-    w_sum = w_sum.reshape(NCTX, PIECE, DM // PIECE)
-
+    lower = lax.axis_index("xh") == 0
+    w_send = jnp.where(lower, w_sum[NZ:], w_sum[:NZ]).astype(BF16)
+    w_sum = jnp.where(lower, w_sum[:NZ], w_sum[NZ:])
+    w_sum = (w_sum + lax.ppermute(w_send, "xh", SWAP).astype(F32)).astype(BF16)
+    outgoing, second = call(
+        outgoing_kernel,
+        [SMEM, VMEM, VMEM],
+        (global_blocks, glob, w_sum.reshape(NZ, PIECE, DM // PIECE)),
+        (shaped((NZ, PIECE, 2 * HALF + DM // PIECE)), shaped((NZ, PIECE, 2 * HALF))),
+    )
+    owned = over_columns(outgoing)
+    second = lax.cond(clash, over_columns, lambda _: nothing, second)
     from_upper = lax.ppermute(to_lower, "z", DOWN)
     from_lower = lax.ppermute(to_upper, "z", UP)
-    kv_other = own[1] + from_upper[1].astype(F32) + from_lower[1].astype(F32)
-    back = lax.ppermute(jnp.concatenate([dq[1], kv_other.astype(BF16)], 1), "xl", SWAP)
-
-    glob = jnp.sum(glob.astype(F32), axis=0).astype(BF16)
-    ids = jnp.arange(NCTX, dtype=jnp.int32)[:, None, None]
-    outgoing = jnp.zeros((NCTX, PIECE, 2 * HALF), BF16)
-    for g in range(NGLOB):
-        part = glob[None, :, g * 2 * HALF : (g + 1) * 2 * HALF]
-        outgoing = jnp.where(ids == global_blocks[g], part, outgoing)
-    owned = lax.all_to_all(
-        jnp.concatenate([outgoing, w_sum], 2), ("xl", "z"), 0, 0, tiled=True
+    kv_mine, back = call(
+        combine_kernel,
+        [SMEM] + [VMEM] * 6,
+        (
+            global_blocks, dq, own, from_upper, from_lower,
+            owned.reshape(BLK, -1), second.reshape(BLK, -1),
+        ),
+        (shaped((BLK, 2 * HALF)), shaped((BLK, 3 * HALF))),
     )
     w_row = jnp.sum(owned[:, :, 2 * HALF :].astype(F32), axis=0).reshape(1, DM)
+    w_row = lax.ppermute(w_row, ("xh", "xl"), CROSS)
     full = shaped((BLK, 2 * HALF))
     query_grad, key_grad, value_grad = call(
         final_kernel,
-        [VMEM] * 6,
-        (dq, own, from_upper, from_lower, back, owned.reshape(2 * BLK, -1)),
+        [VMEM] * 3,
+        (dq, kv_mine, lax.ppermute(back, "xl", SWAP)),
         (full, full, full),
     )
     return query_grad[None], key_grad[None], value_grad[None], w_row

time: 164 us -> 159 us (0.970)
  waiting for transfers between devices: 31 us -> 23.2 us
  between operations: 1.07 us -> 4.93 us
  other arithmetic: 3.77 us -> 0.16 us
  local copies, waits for them, and re-layouts: 4.88 us -> 1.36 us
  starting transfers between devices: 112 us -> 115 us
  Pallas kernels: 8.88 us -> 11.5 us
    ppermute x1, waiting for transfers between devices: 14 us -> 7.51 us  [on_device(): from_upper = lax.ppermute(to_lower, 'z', DOWN)]
    ppermute x2 -> x3, starting transfers between devices: 12.4 us -> 17 us  [the longest x1 9.44 us: on_device(): w_sum = (w_sum + lax.ppermute(w_send, 'xh', SWAP).astype(F32)).astype(BF16)]
    unnamed x26 -> x15, local copies, waits for them, and re-layouts: 4.25 us -> 0.72 us
    ppermute x1, waiting for transfers between devices: 2.77 us -> 0.01 us  [on_device(): lax.ppermute(w_sum[2:].astype(BF16), 'y', Y_TWO).astype(F32)]
    pallas_call x5 -> x7, Pallas kernels: 3.9 us -> 6.51 us  [call(): pl.pallas_call(kernel, out_shape=out_shape, in_specs=specs, out_specs=jax...]
    eq x2 -> x0, other arithmetic: 1.95 us -> none  [on_device(): outgoing = jnp.where(ids == global_blocks[g], part, outgoing)]
    ppermute x1, waiting for transfers between devices: 0.78 us -> 2.68 us  [on_device(): lax.ppermute(w_sum[1].astype(BF16), 'y', Y_ONE).astype(F32)]
    ppermute x2 -> x3, waiting for transfers between devices: 3.81 us -> 2.35 us  [the longest x1 2.34 us: on_device(): lax.ppermute(back, 'xl', SWAP)]
  transfers between devices with their start and end apart: 19 -> 20, of which waited for: 10 -> 9; matrix products, arithmetic and copies ran while one was open for 2% -> 1% of each run, Pallas kernels for 0% -> 0%
where the time goes in v3:
time: 159 us; the launch traced here: 156 us
  starting transfers between devices  115 us (72%)
  waiting for transfers between devices  23.2 us (15%)
  Pallas kernels  11.5 us (7%)
  between operations  4.93 us (3%)
    all_to_all x3, starting transfers between devices, over_columns(): return lax.all_to_all(array.reshape(NZ, PIECE, -1), 'z', 0, 0, tiled=True)  29.8 us
    all_to_all x1, starting transfers between devices, on_device(): lax.all_to_all(halves.reshape(NCTX, PIECE, 2 * HALF), ('xl', 'z'), 0, 0,...  17.1 us
    ppermute x1, starting transfers between devices, on_device(): w_sum = (w_sum + lax.ppermute(w_send, 'xh', SWAP).astype(F32)).astype(BF16)  9.44 us
    ppermute x1, starting transfers between devices, on_device(): lax.ppermute(w_core, 'c', SWAP)  9 us
    ppermute x1, starting transfers between devices, on_device(): w_sum = w_keep + lax.ppermute(w_send, 'c', SWAP).astype(F32)  8.07 us
    ppermute x1, waiting for transfers between devices, on_device(): from_upper = lax.ppermute(to_lower, 'z', DOWN)  7.51 us
    ppermute x1, starting transfers between devices, on_device(): lax.ppermute(back, 'xl', SWAP)  6.94 us
    pallas_call x7, Pallas kernels, call(): pl.pallas_call(kernel, out_shape=out_shape, in_specs=specs, out_specs=jax...  6.51 us
  transfers between devices with their start and end apart: 20, of which 9 were waited for; matrix products, arithmetic and copies ran while one was open for 1% of the time, Pallas kernels for 0%

profile of v3, /device:TPU:1, one launch (start us, length us, event | category | flops | bytes accessed | tf_op | source)
XLA Modules:
  0.0 156.3 jit_solution(16952371939474593091)
XLA Ops:
  0.6 1.9 %shard_map.102 = (bf16[2,128,512]{2,1,0:T(8,128)(2,1)}, bf16[128,768]{1,0:T(8,128)(2,1)}, bf16[128,768]{1,0:T(8,128)(2,1)}) custom-call(bf16[128,512]{1,0:T(8,128)(2,1)} %bitcast.31, bf16[128,512]{1,0:T(8,128)(2,1)} %bitcast.32, bf16[128,512]{1,0:T(8,128)(2,1)} %bitcast.33), custom_call_target="tpu_custom_call" | custom-call | bytes 1048576 | tf_op jit(solution)/shard_map/pallas_call | solution.py:40
  2.5 0.0 copy-start
  2.6 17.1 %all-to-all-start.1 = ((bf16[32,8,512]{2,1,0:T(8,128)(2,1)}), bf16[32,8,512]{2,1,0:T(8,128)(2,1)S(1)}, u32[]{:S(2)}, u32[]{:S(2)}) async-start(bf16[32,8,512]{2,1,0:T(8,128)(2,1)} %bitcast.30), calls=%async_computation.1 | async-start | bytes 524288 | tf_op jit(solution)/shard_map/all_to_all | solution.py:300
  19.7 3.1 %collective-permute-start = (bf16[128,768]{1,0:T(8,128)(2,1)}, bf16[128,768]{1,0:T(8,128)(2,1)S(1)}, u32[]{:S(2)}, u32[]{:S(2)}) collective-permute-start(bf16[128,768]{1,0:T(8,128)(2,1)} %get-tuple-element.29), channel_id=1, source_target_pairs={{0,16},{16,0},{1,17},{17,1},{2,18},{18,2},{3,19},{19,3},{4,20},{20... | collective-permute-start | bytes 589832 | tf_op jit(solution)/shard_map/ppermute | solution.py:303
  22.8 2.1 %collective-permute-start.5 = (bf16[128,1024]{1,0:T(8,128)(2,1)S(1)}, bf16[128,1024]{1,0:T(8,128)(2,1)S(1)}, u32[]{:S(2)}, u32[]{:S(2)}) collective-permute-start(bf16[128,1024]{1,0:T(8,128)(2,1)S(1)} %bitcast.25), channel_id=1, source_target_pairs={{0,16},{16,0},{1,17},{17,1},{2,18},{18,2},{3,19},{19,3},{4,20},{20... | collective-permute-start | bytes 786440 | tf_op jit(solution)/shard_map/ppermute | solution.py:304
  25.0 2.6 %collective-permute-done.other_ref.refs_3_ = bf16[128,768]{1,0:T(8,128)(2,1)S(1)} collective-permute-done((bf16[128,768]{1,0:T(8,128)(2,1)}, bf16[128,768]{1,0:T(8,128)(2,1)S(1)}, u32[]{:S(2)}, u32[]{:S(2)}) %collective-permute-start) | collective-permute-done | bytes 196640 | tf_op jit(solution)/shard_map/ppermute | solution.py:303
  27.6 3.1 %collective-permute-start.1 = (bf16[2,128,512]{2,1,0:T(8,128)(2,1)S(1)}, bf16[2,128,512]{2,1,0:T(8,128)(2,1)S(1)}, u32[]{:S(2)}, u32[]{:S(2)}) collective-permute-start(bf16[2,128,512]{2,1,0:T(8,128)(2,1)S(1)} %shard_map.103), channel_id=1, source_target_pairs={{0,1},{1,2},{2,3},{3,4},{4,5},{5,6},{6,7},{7,8},{8,9},{9,10},{10,1... | collective-permute-start | bytes 786440 | tf_op jit(solution)/shard_map/ppermute | solution.py:308
  30.7 3.6 %collective-permute-start.2 = (bf16[2,128,512]{2,1,0:T(8,128)(2,1)S(1)}, bf16[2,128,512]{2,1,0:T(8,128)(2,1)S(1)}, u32[]{:S(2)}, u32[]{:S(2)}) collective-permute-start(bf16[2,128,512]{2,1,0:T(8,128)(2,1)S(1)} %shard_map.103), channel_id=1, source_target_pairs={{0,15},{1,0},{2,1},{3,2},{4,3},{5,4},{6,5},{7,6},{8,7},{9,8},{10,9... | collective-permute-start | bytes 786440 | tf_op jit(solution)/shard_map/ppermute | solution.py:309
  34.3 0.7 collective-permute-start.3
  34.9 0.0 collective-permute-done.3
  35.0 3.2 %collective-permute-start.4 = (bf16[32,1024]{1,0:T(8,128)(2,1)S(1)}, bf16[32,1024]{1,0:T(8,128)(2,1)S(1)}, u32[]{:S(2)}, u32[]{:S(2)}) collective-permute-start(bf16[32,1024]{1,0:T(8,128)(2,1)S(1)} %collective-permute-done.3), channel_id=1, source_target_pairs={{0,64},{64,0},{128,192},{192,128},{1,65},{65,1},{129,193},{193,129... | collective-permute-start | bytes 196616 | tf_op jit(solution)/shard_map/ppermute | solution.py:306
  38.2 2.1 %collective-permute-done.4.refs_2_ = bf16[32,1024]{1,0:T(8,128)(2,1)S(1)} collective-permute-done((bf16[32,1024]{1,0:T(8,128)(2,1)S(1)}, bf16[32,1024]{1,0:T(8,128)(2,1)S(1)}, u32[]{:S(2)}, u32[]{:S(2)}) %collective-permute-start.4) | collective-permute-done | bytes 65568 | tf_op jit(solution)/shard_map/ppermute | solution.py:306
  40.3 0.0 collective-permute-done.5.refs_3_.grad_other_ref.refs_10_
  40.3 0.0 collective-permute-done.1.refs_0_.refs_4_
  40.3 0.0 collective-permute-done.2.refs_1_.refs_5_
  40.3 0.0 all-to-all-done.1.pieces_ref
  40.3 1.3 shard_map.104
  41.6 11.7 %all-to-all-start.2 = ((bf16[16,8,1536]{2,1,0:T(8,128)(2,1)}), bf16[16,8,1536]{2,1,0:T(8,128)(2,1)S(1)}, u32[]{:S(2)}, u32[]{:S(2)}) async-start(bf16[16,8,1536]{2,1,0:T(8,128)(2,1)} %shard_map.104), calls=%async_computation.2 | async-start | bytes 786432 | tf_op jit(solution)/shard_map/all_to_all | solution.py:279
  53.3 4.8 %collective-permute-start.6 = (bf16[64,1024]{1,0:T(8,128)(2,1)S(1)}, bf16[64,1024]{1,0:T(8,128)(2,1)S(1)}, u32[]{:S(2)}, u32[]{:S(2)}) collective-permute-start(bf16[64,1024]{1,0:T(8,128)(2,1)S(1)} %pad_maximum_fusion), channel_id=1, source_target_pairs={{0,128},{64,192},{128,0},{192,64},{1,129},{65,193},{129,1},{193,65... | collective-permute-start | bytes 393224 | tf_op jit(solution)/shard_map/ppermute | solution.py:318
  58.2 0.0 copy-start.3
  58.2 2.3 %collective-permute-done.6 = bf16[64,1024]{1,0:T(8,128)(2,1)S(1)} collective-permute-done((bf16[64,1024]{1,0:T(8,128)(2,1)S(1)}, bf16[64,1024]{1,0:T(8,128)(2,1)S(1)}, u32[]{:S(2)}, u32[]{:S(2)}) %collective-permute-start.6) | collective-permute-done | bytes 131104 | tf_op jit(solution)/shard_map/ppermute | solution.py:318
  60.6 9.0 %collective-permute-start.7 = (bf16[128,1024]{1,0:T(8,128)(2,1)S(1)}, bf16[128,1024]{1,0:T(8,128)(2,1)S(1)}, u32[]{:S(2)}, u32[]{:S(2)}) collective-permute-start(bf16[128,1024]{1,0:T(8,128)(2,1)S(1)} %constant_dynamic-update-slice_fusion.w_ref), channel_id=1, source_target_pairs={{0,32},{32,0},{1,33},{33,1},{2,34},{34,2},{3,35},{35,3},{4,36},{36... | collective-permute-start | bytes 786440 | tf_op jit(solution)/shard_map/ppermute | solution.py:322
  69.6 0.1 copy.11.refs_0_
  69.7 1.0 collective-permute-done.7.w_other_ref
  70.7 0.5 shard_map.105
  71.2 0.0 all-to-all-done.2
  71.2 5.0 %shard_map.106 = (bf16[2,128,256]{2,1,0:T(8,128)(2,1)S(1)}, f32[2,128,512]{2,1,0:T(8,128)S(1)}, bf16[2,128,512]{2,1,0:T(8,128)(2,1)S(1)}, bf16[2,128,512]{2,1,0:...) custom-call(s32[32,3]{1,0:T(8,128)S(1)} %copy.11.refs_0_, ...), custom_call_target="tpu_custom_call" | custom-call | flops 1000000000 | bytes 5242880 | tf_op jit(solution)/shard_map/pallas_call | solution.py:213
  76.3 8.1 %collective-permute-start.10 = (bf16[4,32,1024]{2,1,0:T(8,128)(2,1)S(1)}, bf16[4,32,1024]{2,1,0:T(8,128)(2,1)S(1)}, u32[]{:S(2)}, u32[]{:S(2)}) collective-permute-start(bf16[4,32,1024]{2,1,0:T(8,128)(2,1)S(1)} %get-tuple-element.39), channel_id=1, source_target_pairs={{0,32},{32,0},{1,33},{33,1},{2,34},{34,2},{3,35},{35,3},{4,36},{36... | collective-permute-start | bytes 786440 | tf_op jit(solution)/shard_map/ppermute | solution.py:333
  84.3 1.1 collective-permute-done.10
  85.5 0.1 convert_add_fusion
  85.6 4.8 %collective-permute-start.11 = (bf16[2,32,1024]{2,1,0:T(8,128)(2,1)S(1)}, bf16[2,32,1024]{2,1,0:T(8,128)(2,1)S(1)}, u32[]{:S(2)}, u32[]{:S(2)}) collective-permute-start(bf16[2,32,1024]{2,1,0:T(8,128)(2,1)S(1)} %slice.71), channel_id=1, source_target_pairs={{0,128},{64,192},{128,0},{192,64},{1,129},{65,193},{129,1},{193,65... | collective-permute-start | bytes 393224 | tf_op jit(solution)/shard_map/ppermute | solution.py:334
  90.4 6.3 %all-to-all-start.3 = ((bf16[16,8,1536]{2,1,0:T(8,128)(2,1)}), bf16[16,8,1536]{2,1,0:T(8,128)(2,1)S(1)}, u32[]{:S(2)}, u32[]{:S(2)}) async-start(bf16[16,8,1536]{2,1,0:T(8,128)(2,1)} %bitcast.7), calls=%async_computation.3 | async-start | bytes 786432 | tf_op jit(solution)/shard_map/all_to_all | solution.py:279
  96.8 2.3 %collective-permute-start.12 = (bf16[32,1024]{1,0:T(8,128)(2,1)S(1)}, bf16[32,1024]{1,0:T(8,128)(2,1)S(1)}, u32[]{:S(2)}, u32[]{:S(2)}) collective-permute-start(bf16[32,1024]{1,0:T(8,128)(2,1)S(1)} %fusion.1), channel_id=1, source_target_pairs={{0,64},{64,0},{128,192},{192,128},{1,65},{65,1},{129,193},{193,129... | collective-permute-start | bytes 196616 | tf_op jit(solution)/shard_map/ppermute | solution.py:335
  99.1 2.7 %collective-permute-done.12 = bf16[32,1024]{1,0:T(8,128)(2,1)S(1)} collective-permute-done((bf16[32,1024]{1,0:T(8,128)(2,1)S(1)}, bf16[32,1024]{1,0:T(8,128)(2,1)S(1)}, u32[]{:S(2)}, u32[]{:S(2)}) %collective-permute-start.12) | collective-permute-done | bytes 65568 | tf_op jit(solution)/shard_map/ppermute | solution.py:335
  101.8 9.4 %collective-permute-start.13 = (bf16[16,1024]{1,0:T(8,128)(2,1)S(1)}, bf16[16,1024]{1,0:T(8,128)(2,1)S(1)}, u32[]{:S(2)}, u32[]{:S(2)}) collective-permute-start(bf16[16,1024]{1,0:T(8,128)(2,1)S(1)} %select_convert_fusion), channel_id=1, source_target_pairs={{0,256},{256,0},{1,257},{257,1},{2,258},{258,2},{3,259},{259,3},{4... | collective-permute-start | bytes 98312 | tf_op jit(solution)/shard_map/ppermute | solution.py:339
  111.3 0.6 fusion.4
  115.8 1.3 shard_map.107
  117.1 11.8 %all-to-all-start.4 = ((bf16[16,8,640]{2,1,0:T(8,128)(2,1)}), bf16[16,8,640]{2,1,0:T(8,128)(2,1)S(1)}, u32[]{:S(2)}, u32[]{:S(2)}) async-start(bf16[16,8,640]{2,1,0:T(8,128)(2,1)} %get-tuple-element.40), calls=%async_computation.4 | async-start | bytes 327680 | tf_op jit(solution)/shard_map/all_to_all | solution.py:279
  128.9 4.5 %collective-permute-start.8 = (bf16[2,128,512]{2,1,0:T(8,128)(2,1)S(1)}, bf16[2,128,512]{2,1,0:T(8,128)(2,1)S(1)}, u32[]{:S(2)}, u32[]{:S(2)}) collective-permute-start(bf16[2,128,512]{2,1,0:T(8,128)(2,1)S(1)} %get-tuple-element.35), channel_id=1, source_target_pairs={{0,15},{1,0},{2,1},{3,2},{4,3},{5,4},{6,5},{7,6},{8,7},{9,8},{10,9... | collective-permute-start | bytes 786440 | tf_op jit(solution)/shard_map/ppermute | solution.py:348
  133.4 1.9 %collective-permute-start.9 = (bf16[2,128,512]{2,1,0:T(8,128)(2,1)S(1)}, bf16[2,128,512]{2,1,0:T(8,128)(2,1)S(1)}, u32[]{:S(2)}, u32[]{:S(2)}) collective-permute-start(bf16[2,128,512]{2,1,0:T(8,128)(2,1)S(1)} %get-tuple-element.36), channel_id=1, source_target_pairs={{0,1},{1,2},{2,3},{3,4},{4,5},{5,6},{6,7},{7,8},{8,9},{9,10},{10,1... | collective-permute-start | bytes 786440 | tf_op jit(solution)/shard_map/ppermute | solution.py:349
  135.3 7.5 %collective-permute-done.8.upper_ref = bf16[2,128,512]{2,1,0:T(8,128)(2,1)S(1)} collective-permute-done((bf16[2,128,512]{2,1,0:T(8,128)(2,1)S(1)}, bf16[2,128,512]{2,1,0:T(8,128)(2,1)S(1)}, u32[]{:S(2)}, u32[]{:S(2)}) %collective-permute-start.8) | collective-permute-done | bytes 262176 | tf_op jit(solution)/shard_map/ppermute | solution.py:348
  142.8 1.4 collective-permute-done.9.lower_ref
  144.2 0.7 shard_map.108
  145.0 6.9 %collective-permute-start.14 = (bf16[128,768]{1,0:T(8,128)(2,1)S(1)}, bf16[128,768]{1,0:T(8,128)(2,1)S(1)}, u32[]{:S(2)}, u32[]{:S(2)}) collective-permute-start(bf16[128,768]{1,0:T(8,128)(2,1)S(1)} %get-tuple-element.43), channel_id=1, source_target_pairs={{0,16},{16,0},{1,17},{17,1},{2,18},{18,2},{3,19},{19,3},{4,20},{20... | collective-permute-start | bytes 589832 | tf_op jit(solution)/shard_map/ppermute | solution.py:365
  151.9 0.7 collective-permute-start.15
  152.6 2.3 %collective-permute-done.14.back_ref = bf16[128,768]{1,0:T(8,128)(2,1)S(1)} collective-permute-done((bf16[128,768]{1,0:T(8,128)(2,1)S(1)}, bf16[128,768]{1,0:T(8,128)(2,1)S(1)}, u32[]{:S(2)}, u32[]{:S(2)}) %collective-permute-start.14) | collective-permute-done | bytes 196640 | tf_op jit(solution)/shard_map/ppermute | solution.py:365
  155.0 0.8 shard_map.109
  155.7 0.6 copy.18
  (29 shorter events, 0.2 us)
Async XLA Ops:
  2.5 20.3 %copy-start = (bf16[1,128,1024]{2,1,0:T(8,128)(2,1)S(1)}, bf16[1,128,1024]{2,1,0:T(8,128)(2,1)}, u32[]{:S(2)}) copy-start(bf16[1,128,1024]{2,1,0:T(8,128)(2,1)} %param.12) | copy-start | bytes 786436
  2.5 25.0 %copy-start.1 = (bf16[128,768]{1,0:T(8,128)(2,1)S(1)}, bf16[128,768]{1,0:T(8,128)(2,1)}, u32[]{:S(2)}) copy-start(bf16[128,768]{1,0:T(8,128)(2,1)} %get-tuple-element.28.mine_ref.refs_2_) | copy-start | bytes 589828
  2.6 37.7 %all-to-all-start.1 = ((bf16[32,8,512]{2,1,0:T(8,128)(2,1)}), bf16[32,8,512]{2,1,0:T(8,128)(2,1)S(1)}, u32[]{:S(2)}, u32[]{:S(2)}) async-start(bf16[32,8,512]{2,1,0:T(8,128)(2,1)} %bitcast.30), calls=%async_computation.1 | async-start | bytes 524288 | tf_op jit(solution)/shard_map/all_to_all | solution.py:300
  19.7 7.9 %collective-permute-start = (bf16[128,768]{1,0:T(8,128)(2,1)}, bf16[128,768]{1,0:T(8,128)(2,1)S(1)}, u32[]{:S(2)}, u32[]{:S(2)}) collective-permute-start(bf16[128,768]{1,0:T(8,128)(2,1)} %get-tuple-element.29), channel_id=1, source_target_pairs={{0,16},{16,0},{1,17},{17,1},{2,18},{18,2},{3,19},{19,3},{4,20},{20... | collective-permute-start | bytes 589832 | tf_op jit(solution)/shard_map/ppermute | solution.py:303
  22.8 17.4 %collective-permute-start.5 = (bf16[128,1024]{1,0:T(8,128)(2,1)S(1)}, bf16[128,1024]{1,0:T(8,128)(2,1)S(1)}, u32[]{:S(2)}, u32[]{:S(2)}) collective-permute-start(bf16[128,1024]{1,0:T(8,128)(2,1)S(1)} %bitcast.25), channel_id=1, source_target_pairs={{0,16},{16,0},{1,17},{17,1},{2,18},{18,2},{3,19},{19,3},{4,20},{20... | collective-permute-start | bytes 786440 | tf_op jit(solution)/shard_map/ppermute | solution.py:304
  27.6 6.7 %copy-start.4 = (bf16[32,1024]{1,0:T(8,128)(2,1)S(1)}, bf16[32,1024]{1,0:T(8,128)(2,1)}, u32[]{:S(2)}) copy-start(bf16[32,1024]{1,0:T(8,128)(2,1)} %param.13) | copy-start | bytes 196612
  27.6 12.7 %copy-start.2 = (s32[3]{0:T(128)S(1)}, s32[3]{0:T(128)}, u32[]{:S(2)}) copy-start(s32[3]{0:T(128)} %globals_ref.5) | copy-start | bytes 40
  27.6 12.7 %collective-permute-start.1 = (bf16[2,128,512]{2,1,0:T(8,128)(2,1)S(1)}, bf16[2,128,512]{2,1,0:T(8,128)(2,1)S(1)}, u32[]{:S(2)}, u32[]{:S(2)}) collective-permute-start(bf16[2,128,512]{2,1,0:T(8,128)(2,1)S(1)} %shard_map.103), channel_id=1, source_target_pairs={{0,1},{1,2},{2,3},{3,4},{4,5},{5,6},{6,7},{7,8},{8,9},{9,10},{10,1... | collective-permute-start | bytes 786440 | tf_op jit(solution)/shard_map/ppermute | solution.py:308
  30.7 9.6 %collective-permute-start.2 = (bf16[2,128,512]{2,1,0:T(8,128)(2,1)S(1)}, bf16[2,128,512]{2,1,0:T(8,128)(2,1)S(1)}, u32[]{:S(2)}, u32[]{:S(2)}) collective-permute-start(bf16[2,128,512]{2,1,0:T(8,128)(2,1)S(1)} %shard_map.103), channel_id=1, source_target_pairs={{0,15},{1,0},{2,1},{3,2},{4,3},{5,4},{6,5},{7,6},{8,7},{9,8},{10,9... | collective-permute-start | bytes 786440 | tf_op jit(solution)/shard_map/ppermute | solution.py:309
  34.3 0.7 collective-permute-start.3
  35.0 5.3 %collective-permute-start.4 = (bf16[32,1024]{1,0:T(8,128)(2,1)S(1)}, bf16[32,1024]{1,0:T(8,128)(2,1)S(1)}, u32[]{:S(2)}, u32[]{:S(2)}) collective-permute-start(bf16[32,1024]{1,0:T(8,128)(2,1)S(1)} %collective-permute-done.3), channel_id=1, source_target_pairs={{0,64},{64,0},{128,192},{192,128},{1,65},{65,1},{129,193},{193,129... | collective-permute-start | bytes 196616 | tf_op jit(solution)/shard_map/ppermute | solution.py:306
  41.6 29.6 %all-to-all-start.2 = ((bf16[16,8,1536]{2,1,0:T(8,128)(2,1)}), bf16[16,8,1536]{2,1,0:T(8,128)(2,1)S(1)}, u32[]{:S(2)}, u32[]{:S(2)}) async-start(bf16[16,8,1536]{2,1,0:T(8,128)(2,1)} %shard_map.104), calls=%async_computation.2 | async-start | bytes 786432 | tf_op jit(solution)/shard_map/all_to_all | solution.py:279
  53.3 7.2 %collective-permute-start.6 = (bf16[64,1024]{1,0:T(8,128)(2,1)S(1)}, bf16[64,1024]{1,0:T(8,128)(2,1)S(1)}, u32[]{:S(2)}, u32[]{:S(2)}) collective-permute-start(bf16[64,1024]{1,0:T(8,128)(2,1)S(1)} %pad_maximum_fusion), channel_id=1, source_target_pairs={{0,128},{64,192},{128,0},{192,64},{1,129},{65,193},{129,1},{193,65... | collective-permute-start | bytes 393224 | tf_op jit(solution)/shard_map/ppermute | solution.py:318
  58.2 11.4 %copy-start.3 = (s32[32,3]{0,1:T(4,128)S(1)}, s32[32,3]{0,1:T(4,128)}, u32[]{:S(2)}) copy-start(s32[32,3]{0,1:T(4,128)} %param.14) | copy-start | bytes 1156
  60.6 10.2 %collective-permute-start.7 = (bf16[128,1024]{1,0:T(8,128)(2,1)S(1)}, bf16[128,1024]{1,0:T(8,128)(2,1)S(1)}, u32[]{:S(2)}, u32[]{:S(2)}) collective-permute-start(bf16[128,1024]{1,0:T(8,128)(2,1)S(1)} %constant_dynamic-update-slice_fusion.w_ref), channel_id=1, source_target_pairs={{0,32},{32,0},{1,33},{33,1},{2,34},{34,2},{3,35},{35,3},{4,36},{36... | collective-permute-start | bytes 786440 | tf_op jit(solution)/shard_map/ppermute | solution.py:322
  76.3 9.2 %collective-permute-start.10 = (bf16[4,32,1024]{2,1,0:T(8,128)(2,1)S(1)}, bf16[4,32,1024]{2,1,0:T(8,128)(2,1)S(1)}, u32[]{:S(2)}, u32[]{:S(2)}) collective-permute-start(bf16[4,32,1024]{2,1,0:T(8,128)(2,1)S(1)} %get-tuple-element.39), channel_id=1, source_target_pairs={{0,32},{32,0},{1,33},{33,1},{2,34},{34,2},{3,35},{35,3},{4,36},{36... | collective-permute-start | bytes 786440 | tf_op jit(solution)/shard_map/ppermute | solution.py:333
  85.6 11.2 %collective-permute-start.11 = (bf16[2,32,1024]{2,1,0:T(8,128)(2,1)S(1)}, bf16[2,32,1024]{2,1,0:T(8,128)(2,1)S(1)}, u32[]{:S(2)}, u32[]{:S(2)}) collective-permute-start(bf16[2,32,1024]{2,1,0:T(8,128)(2,1)S(1)} %slice.71), channel_id=1, source_target_pairs={{0,128},{64,192},{128,0},{192,64},{1,129},{65,193},{129,1},{193,65... | collective-permute-start | bytes 393224 | tf_op jit(solution)/shard_map/ppermute | solution.py:334
  90.4 25.4 %all-to-all-start.3 = ((bf16[16,8,1536]{2,1,0:T(8,128)(2,1)}), bf16[16,8,1536]{2,1,0:T(8,128)(2,1)S(1)}, u32[]{:S(2)}, u32[]{:S(2)}) async-start(bf16[16,8,1536]{2,1,0:T(8,128)(2,1)} %bitcast.7), calls=%async_computation.3 | async-start | bytes 786432 | tf_op jit(solution)/shard_map/all_to_all | solution.py:279
  96.8 5.0 %collective-permute-start.12 = (bf16[32,1024]{1,0:T(8,128)(2,1)S(1)}, bf16[32,1024]{1,0:T(8,128)(2,1)S(1)}, u32[]{:S(2)}, u32[]{:S(2)}) collective-permute-start(bf16[32,1024]{1,0:T(8,128)(2,1)S(1)} %fusion.1), channel_id=1, source_target_pairs={{0,64},{64,0},{128,192},{192,128},{1,65},{65,1},{129,193},{193,129... | collective-permute-start | bytes 196616 | tf_op jit(solution)/shard_map/ppermute | solution.py:335
  101.8 13.9 %collective-permute-start.13 = (bf16[16,1024]{1,0:T(8,128)(2,1)S(1)}, bf16[16,1024]{1,0:T(8,128)(2,1)S(1)}, u32[]{:S(2)}, u32[]{:S(2)}) collective-permute-start(bf16[16,1024]{1,0:T(8,128)(2,1)S(1)} %select_convert_fusion), channel_id=1, source_target_pairs={{0,256},{256,0},{1,257},{257,1},{2,258},{258,2},{3,259},{259,3},{4... | collective-permute-start | bytes 98312 | tf_op jit(solution)/shard_map/ppermute | solution.py:339
  117.1 27.1 %all-to-all-start.4 = ((bf16[16,8,640]{2,1,0:T(8,128)(2,1)}), bf16[16,8,640]{2,1,0:T(8,128)(2,1)S(1)}, u32[]{:S(2)}, u32[]{:S(2)}) async-start(bf16[16,8,640]{2,1,0:T(8,128)(2,1)} %get-tuple-element.40), calls=%async_computation.4 | async-start | bytes 327680 | tf_op jit(solution)/shard_map/all_to_all | solution.py:279
  128.9 13.9 %collective-permute-start.8 = (bf16[2,128,512]{2,1,0:T(8,128)(2,1)S(1)}, bf16[2,128,512]{2,1,0:T(8,128)(2,1)S(1)}, u32[]{:S(2)}, u32[]{:S(2)}) collective-permute-start(bf16[2,128,512]{2,1,0:T(8,128)(2,1)S(1)} %get-tuple-element.35), channel_id=1, source_target_pairs={{0,15},{1,0},{2,1},{3,2},{4,3},{5,4},{6,5},{7,6},{8,7},{9,8},{10,9... | collective-permute-start | bytes 786440 | tf_op jit(solution)/shard_map/ppermute | solution.py:348
  133.4 10.8 %collective-permute-start.9 = (bf16[2,128,512]{2,1,0:T(8,128)(2,1)S(1)}, bf16[2,128,512]{2,1,0:T(8,128)(2,1)S(1)}, u32[]{:S(2)}, u32[]{:S(2)}) collective-permute-start(bf16[2,128,512]{2,1,0:T(8,128)(2,1)S(1)} %get-tuple-element.36), channel_id=1, source_target_pairs={{0,1},{1,2},{2,3},{3,4},{4,5},{5,6},{6,7},{7,8},{8,9},{9,10},{10,1... | collective-permute-start | bytes 786440 | tf_op jit(solution)/shard_map/ppermute | solution.py:349
  145.0 10.0 %collective-permute-start.14 = (bf16[128,768]{1,0:T(8,128)(2,1)S(1)}, bf16[128,768]{1,0:T(8,128)(2,1)S(1)}, u32[]{:S(2)}, u32[]{:S(2)}) collective-permute-start(bf16[128,768]{1,0:T(8,128)(2,1)S(1)} %get-tuple-element.43), channel_id=1, source_target_pairs={{0,16},{16,0},{1,17},{17,1},{2,18},{18,2},{3,19},{19,3},{4,20},{20... | collective-permute-start | bytes 589832 | tf_op jit(solution)/shard_map/ppermute | solution.py:365
  151.9 0.7 collective-permute-start.15

commit v4 on v3

--- a/solution.py
+++ b/solution.py
@@ -265,7 +265,8 @@
             back_ref[:, :HALF] = dq_ref[1]
 
 
-def final_kernel(dq_ref, kv_ref, back_ref, q_ref, k_ref, v_ref):
+def final_kernel(dq_ref, kv_ref, back_ref, w_ref, q_ref, k_ref, v_ref, w_out_ref):
+    w_out_ref[...] = w_ref[...]
     first = lax.axis_index("xl") == 0
     for half in range(2):
         mine = first if half == 0 else jnp.logical_not(first)
@@ -356,16 +357,16 @@
         ),
         (shaped((BLK, 2 * HALF)), shaped((BLK, 3 * HALF))),
     )
-    w_row = jnp.sum(owned[:, :, 2 * HALF :].astype(F32), axis=0).reshape(1, DM)
+    w_row = jnp.sum(owned[:, :, 2 * HALF :].astype(F32), axis=0)
     w_row = lax.ppermute(w_row, ("xh", "xl"), CROSS)
     full = shaped((BLK, 2 * HALF))
-    query_grad, key_grad, value_grad = call(
+    query_grad, key_grad, value_grad, w_row = call(
         final_kernel,
-        [VMEM] * 3,
-        (dq, kv_mine, lax.ppermute(back, "xl", SWAP)),
-        (full, full, full),
-    )
-    return query_grad[None], key_grad[None], value_grad[None], w_row
+        [VMEM] * 4,
+        (dq, kv_mine, lax.ppermute(back, "xl", SWAP), w_row),
+        (full, full, full, shaped(w_row.shape, F32)),
+    )
+    return query_grad[None], key_grad[None], value_grad[None], w_row.reshape(1, DM)
 
 
 def solution(mesh):

time: 159 us -> 159 us (level)
  no operation moved by 1% of the time
where the time goes in v4:
time: 159 us; the launch traced here: 156 us
  starting transfers between devices  115 us (72%)
  waiting for transfers between devices  23.2 us (15%)
  Pallas kernels  11.5 us (7%)
  between operations  4.93 us (3%)
    all_to_all x3, starting transfers between devices, over_columns(): return lax.all_to_all(array.reshape(NZ, PIECE, -1), 'z', 0, 0, tiled=True)  29.8 us
    all_to_all x1, starting transfers between devices, on_device(): lax.all_to_all(halves.reshape(NCTX, PIECE, 2 * HALF), ('xl', 'z'), 0, 0,...  17.1 us
    ppermute x1, starting transfers between devices, on_device(): w_sum = (w_sum + lax.ppermute(w_send, 'xh', SWAP).astype(F32)).astype(BF16)  9.44 us
    ppermute x1, starting transfers between devices, on_device(): lax.ppermute(w_core, 'c', SWAP)  9 us
    ppermute x1, starting transfers between devices, on_device(): w_sum = w_keep + lax.ppermute(w_send, 'c', SWAP).astype(F32)  8.05 us
    ppermute x1, waiting for transfers between devices, on_device(): from_upper = lax.ppermute(to_lower, 'z', DOWN)  7.51 us
    ppermute x1, starting transfers between devices, on_device(): lax.ppermute(back, 'xl', SWAP)  6.94 us
    pallas_call x7, Pallas kernels, call(): pl.pallas_call(kernel, out_shape=out_shape, in_specs=specs, out_specs=jax...  6.51 us
  transfers between devices with their start and end apart: 20, of which 9 were waited for; matrix products, arithmetic and copies ran while one was open for 1% of the time, Pallas kernels for 0%

profile of v4, /device:TPU:1, one launch (start us, length us, event | category | flops | bytes accessed | tf_op | source)
XLA Modules:
  0.0 155.7 jit_solution(7596692715944694812)
XLA Ops:
  0.6 1.9 %shard_map.102 = (bf16[2,128,512]{2,1,0:T(8,128)(2,1)}, bf16[128,768]{1,0:T(8,128)(2,1)}, bf16[128,768]{1,0:T(8,128)(2,1)}) custom-call(bf16[128,512]{1,0:T(8,128)(2,1)} %bitcast.31, bf16[128,512]{1,0:T(8,128)(2,1)} %bitcast.32, bf16[128,512]{1,0:T(8,128)(2,1)} %bitcast.33), custom_call_target="tpu_custom_call" | custom-call | bytes 1048576 | tf_op jit(solution)/shard_map/pallas_call | solution.py:40
  2.5 0.0 copy-start
  2.6 17.1 %all-to-all-start.1 = ((bf16[32,8,512]{2,1,0:T(8,128)(2,1)}), bf16[32,8,512]{2,1,0:T(8,128)(2,1)S(1)}, u32[]{:S(2)}, u32[]{:S(2)}) async-start(bf16[32,8,512]{2,1,0:T(8,128)(2,1)} %bitcast.30), calls=%async_computation.1 | async-start | bytes 524288 | tf_op jit(solution)/shard_map/all_to_all | solution.py:301
  19.7 3.1 %collective-permute-start = (bf16[128,768]{1,0:T(8,128)(2,1)}, bf16[128,768]{1,0:T(8,128)(2,1)S(1)}, u32[]{:S(2)}, u32[]{:S(2)}) collective-permute-start(bf16[128,768]{1,0:T(8,128)(2,1)} %get-tuple-element.30), channel_id=1, source_target_pairs={{0,16},{16,0},{1,17},{17,1},{2,18},{18,2},{3,19},{19,3},{4,20},{20... | collective-permute-start | bytes 589832 | tf_op jit(solution)/shard_map/ppermute | solution.py:304
  22.8 2.1 %collective-permute-start.5 = (bf16[128,1024]{1,0:T(8,128)(2,1)S(1)}, bf16[128,1024]{1,0:T(8,128)(2,1)S(1)}, u32[]{:S(2)}, u32[]{:S(2)}) collective-permute-start(bf16[128,1024]{1,0:T(8,128)(2,1)S(1)} %bitcast.25), channel_id=1, source_target_pairs={{0,16},{16,0},{1,17},{17,1},{2,18},{18,2},{3,19},{19,3},{4,20},{20... | collective-permute-start | bytes 786440 | tf_op jit(solution)/shard_map/ppermute | solution.py:305
  25.0 2.6 %collective-permute-done.other_ref.refs_3_ = bf16[128,768]{1,0:T(8,128)(2,1)S(1)} collective-permute-done((bf16[128,768]{1,0:T(8,128)(2,1)}, bf16[128,768]{1,0:T(8,128)(2,1)S(1)}, u32[]{:S(2)}, u32[]{:S(2)}) %collective-permute-start) | collective-permute-done | bytes 196640 | tf_op jit(solution)/shard_map/ppermute | solution.py:304
  27.6 3.1 %collective-permute-start.1 = (bf16[2,128,512]{2,1,0:T(8,128)(2,1)S(1)}, bf16[2,128,512]{2,1,0:T(8,128)(2,1)S(1)}, u32[]{:S(2)}, u32[]{:S(2)}) collective-permute-start(bf16[2,128,512]{2,1,0:T(8,128)(2,1)S(1)} %shard_map.103), channel_id=1, source_target_pairs={{0,1},{1,2},{2,3},{3,4},{4,5},{5,6},{6,7},{7,8},{8,9},{9,10},{10,1... | collective-permute-start | bytes 786440 | tf_op jit(solution)/shard_map/ppermute | solution.py:309
  30.7 3.6 %collective-permute-start.2 = (bf16[2,128,512]{2,1,0:T(8,128)(2,1)S(1)}, bf16[2,128,512]{2,1,0:T(8,128)(2,1)S(1)}, u32[]{:S(2)}, u32[]{:S(2)}) collective-permute-start(bf16[2,128,512]{2,1,0:T(8,128)(2,1)S(1)} %shard_map.103), channel_id=1, source_target_pairs={{0,15},{1,0},{2,1},{3,2},{4,3},{5,4},{6,5},{7,6},{8,7},{9,8},{10,9... | collective-permute-start | bytes 786440 | tf_op jit(solution)/shard_map/ppermute | solution.py:310
  34.3 0.7 collective-permute-start.3
  34.9 0.0 collective-permute-done.3
  35.0 3.2 %collective-permute-start.4 = (bf16[32,1024]{1,0:T(8,128)(2,1)S(1)}, bf16[32,1024]{1,0:T(8,128)(2,1)S(1)}, u32[]{:S(2)}, u32[]{:S(2)}) collective-permute-start(bf16[32,1024]{1,0:T(8,128)(2,1)S(1)} %collective-permute-done.3), channel_id=1, source_target_pairs={{0,64},{64,0},{128,192},{192,128},{1,65},{65,1},{129,193},{193,129... | collective-permute-start | bytes 196616 | tf_op jit(solution)/shard_map/ppermute | solution.py:307
  38.2 2.1 %collective-permute-done.4.refs_2_ = bf16[32,1024]{1,0:T(8,128)(2,1)S(1)} collective-permute-done((bf16[32,1024]{1,0:T(8,128)(2,1)S(1)}, bf16[32,1024]{1,0:T(8,128)(2,1)S(1)}, u32[]{:S(2)}, u32[]{:S(2)}) %collective-permute-start.4) | collective-permute-done | bytes 65568 | tf_op jit(solution)/shard_map/ppermute | solution.py:307
  40.3 0.0 collective-permute-done.5.refs_3_.grad_other_ref.refs_10_
  40.3 0.0 collective-permute-done.1.refs_0_.refs_4_
  40.3 0.0 collective-permute-done.2.refs_1_.refs_5_
  40.3 0.0 all-to-all-done.1.pieces_ref
  40.3 1.3 shard_map.104
  41.6 11.7 %all-to-all-start.2 = ((bf16[16,8,1536]{2,1,0:T(8,128)(2,1)}), bf16[16,8,1536]{2,1,0:T(8,128)(2,1)S(1)}, u32[]{:S(2)}, u32[]{:S(2)}) async-start(bf16[16,8,1536]{2,1,0:T(8,128)(2,1)} %shard_map.104), calls=%async_computation.2 | async-start | bytes 786432 | tf_op jit(solution)/shard_map/all_to_all | solution.py:280
  53.3 4.8 %collective-permute-start.6 = (bf16[64,1024]{1,0:T(8,128)(2,1)S(1)}, bf16[64,1024]{1,0:T(8,128)(2,1)S(1)}, u32[]{:S(2)}, u32[]{:S(2)}) collective-permute-start(bf16[64,1024]{1,0:T(8,128)(2,1)S(1)} %pad_maximum_fusion), channel_id=1, source_target_pairs={{0,128},{64,192},{128,0},{192,64},{1,129},{65,193},{129,1},{193,65... | collective-permute-start | bytes 393224 | tf_op jit(solution)/shard_map/ppermute | solution.py:319
  58.2 0.0 copy-start.3
  58.2 2.3 %collective-permute-done.6 = bf16[64,1024]{1,0:T(8,128)(2,1)S(1)} collective-permute-done((bf16[64,1024]{1,0:T(8,128)(2,1)S(1)}, bf16[64,1024]{1,0:T(8,128)(2,1)S(1)}, u32[]{:S(2)}, u32[]{:S(2)}) %collective-permute-start.6) | collective-permute-done | bytes 131104 | tf_op jit(solution)/shard_map/ppermute | solution.py:319
  60.6 9.0 %collective-permute-start.7 = (bf16[128,1024]{1,0:T(8,128)(2,1)S(1)}, bf16[128,1024]{1,0:T(8,128)(2,1)S(1)}, u32[]{:S(2)}, u32[]{:S(2)}) collective-permute-start(bf16[128,1024]{1,0:T(8,128)(2,1)S(1)} %constant_dynamic-update-slice_fusion.w_ref), channel_id=1, source_target_pairs={{0,32},{32,0},{1,33},{33,1},{2,34},{34,2},{3,35},{35,3},{4,36},{36... | collective-permute-start | bytes 786440 | tf_op jit(solution)/shard_map/ppermute | solution.py:323
  69.6 0.1 copy.11.refs_0_
  69.7 1.0 collective-permute-done.7.w_other_ref
  70.7 0.5 shard_map.105
  71.2 0.0 all-to-all-done.2
  71.2 5.0 %shard_map.106 = (bf16[2,128,256]{2,1,0:T(8,128)(2,1)S(1)}, f32[2,128,512]{2,1,0:T(8,128)S(1)}, bf16[2,128,512]{2,1,0:T(8,128)(2,1)S(1)}, bf16[2,128,512]{2,1,0:...) custom-call(s32[32,3]{1,0:T(8,128)S(1)} %copy.11.refs_0_, ...), custom_call_target="tpu_custom_call" | custom-call | flops 1000000000 | bytes 5242880 | tf_op jit(solution)/shard_map/pallas_call | solution.py:213
  76.3 8.1 %collective-permute-start.10 = (bf16[4,32,1024]{2,1,0:T(8,128)(2,1)S(1)}, bf16[4,32,1024]{2,1,0:T(8,128)(2,1)S(1)}, u32[]{:S(2)}, u32[]{:S(2)}) collective-permute-start(bf16[4,32,1024]{2,1,0:T(8,128)(2,1)S(1)} %get-tuple-element.40), channel_id=1, source_target_pairs={{0,32},{32,0},{1,33},{33,1},{2,34},{34,2},{3,35},{35,3},{4,36},{36... | collective-permute-start | bytes 786440 | tf_op jit(solution)/shard_map/ppermute | solution.py:334
  84.3 1.1 collective-permute-done.10
  85.5 0.1 convert_add_fusion
  85.6 4.8 %collective-permute-start.11 = (bf16[2,32,1024]{2,1,0:T(8,128)(2,1)S(1)}, bf16[2,32,1024]{2,1,0:T(8,128)(2,1)S(1)}, u32[]{:S(2)}, u32[]{:S(2)}) collective-permute-start(bf16[2,32,1024]{2,1,0:T(8,128)(2,1)S(1)} %slice.71), channel_id=1, source_target_pairs={{0,128},{64,192},{128,0},{192,64},{1,129},{65,193},{129,1},{193,65... | collective-permute-start | bytes 393224 | tf_op jit(solution)/shard_map/ppermute | solution.py:335
  90.4 6.3 %all-to-all-start.3 = ((bf16[16,8,1536]{2,1,0:T(8,128)(2,1)}), bf16[16,8,1536]{2,1,0:T(8,128)(2,1)S(1)}, u32[]{:S(2)}, u32[]{:S(2)}) async-start(bf16[16,8,1536]{2,1,0:T(8,128)(2,1)} %bitcast.7), calls=%async_computation.3 | async-start | bytes 786432 | tf_op jit(solution)/shard_map/all_to_all | solution.py:280
  96.8 0.0 collective-permute-done.11
  96.8 2.3 %collective-permute-start.12 = (bf16[32,1024]{1,0:T(8,128)(2,1)S(1)}, bf16[32,1024]{1,0:T(8,128)(2,1)S(1)}, u32[]{:S(2)}, u32[]{:S(2)}) collective-permute-start(bf16[32,1024]{1,0:T(8,128)(2,1)S(1)} %fusion.1), channel_id=1, source_target_pairs={{0,64},{64,0},{128,192},{192,128},{1,65},{65,1},{129,193},{193,129... | collective-permute-start | bytes 196616 | tf_op jit(solution)/shard_map/ppermute | solution.py:336
  99.1 2.7 %collective-permute-done.12 = bf16[32,1024]{1,0:T(8,128)(2,1)S(1)} collective-permute-done((bf16[32,1024]{1,0:T(8,128)(2,1)S(1)}, bf16[32,1024]{1,0:T(8,128)(2,1)S(1)}, u32[]{:S(2)}, u32[]{:S(2)}) %collective-permute-start.12) | collective-permute-done | bytes 65568 | tf_op jit(solution)/shard_map/ppermute | solution.py:336
  101.9 9.4 %collective-permute-start.13 = (bf16[16,1024]{1,0:T(8,128)(2,1)S(1)}, bf16[16,1024]{1,0:T(8,128)(2,1)S(1)}, u32[]{:S(2)}, u32[]{:S(2)}) collective-permute-start(bf16[16,1024]{1,0:T(8,128)(2,1)S(1)} %select_convert_fusion), channel_id=1, source_target_pairs={{0,256},{256,0},{1,257},{257,1},{2,258},{258,2},{3,259},{259,3},{4... | collective-permute-start | bytes 98312 | tf_op jit(solution)/shard_map/ppermute | solution.py:340
  111.3 0.6 fusion.4
  115.8 1.3 shard_map.107
  117.2 11.8 %all-to-all-start.4 = ((bf16[16,8,640]{2,1,0:T(8,128)(2,1)}), bf16[16,8,640]{2,1,0:T(8,128)(2,1)S(1)}, u32[]{:S(2)}, u32[]{:S(2)}) async-start(bf16[16,8,640]{2,1,0:T(8,128)(2,1)} %get-tuple-element.41), calls=%async_computation.4 | async-start | bytes 327680 | tf_op jit(solution)/shard_map/all_to_all | solution.py:280
  128.9 4.5 %collective-permute-start.8 = (bf16[2,128,512]{2,1,0:T(8,128)(2,1)S(1)}, bf16[2,128,512]{2,1,0:T(8,128)(2,1)S(1)}, u32[]{:S(2)}, u32[]{:S(2)}) collective-permute-start(bf16[2,128,512]{2,1,0:T(8,128)(2,1)S(1)} %get-tuple-element.36), channel_id=1, source_target_pairs={{0,15},{1,0},{2,1},{3,2},{4,3},{5,4},{6,5},{7,6},{8,7},{9,8},{10,9... | collective-permute-start | bytes 786440 | tf_op jit(solution)/shard_map/ppermute | solution.py:349
  133.4 1.9 %collective-permute-start.9 = (bf16[2,128,512]{2,1,0:T(8,128)(2,1)S(1)}, bf16[2,128,512]{2,1,0:T(8,128)(2,1)S(1)}, u32[]{:S(2)}, u32[]{:S(2)}) collective-permute-start(bf16[2,128,512]{2,1,0:T(8,128)(2,1)S(1)} %get-tuple-element.37), channel_id=1, source_target_pairs={{0,1},{1,2},{2,3},{3,4},{4,5},{5,6},{6,7},{7,8},{8,9},{9,10},{10,1... | collective-permute-start | bytes 786440 | tf_op jit(solution)/shard_map/ppermute | solution.py:350
  135.3 7.5 %collective-permute-done.8.upper_ref = bf16[2,128,512]{2,1,0:T(8,128)(2,1)S(1)} collective-permute-done((bf16[2,128,512]{2,1,0:T(8,128)(2,1)S(1)}, bf16[2,128,512]{2,1,0:T(8,128)(2,1)S(1)}, u32[]{:S(2)}, u32[]{:S(2)}) %collective-permute-start.8) | collective-permute-done | bytes 262176 | tf_op jit(solution)/shard_map/ppermute | solution.py:349
  142.9 1.4 collective-permute-done.9.lower_ref
  144.2 0.7 shard_map.108
  145.0 6.9 %collective-permute-start.14 = (bf16[128,768]{1,0:T(8,128)(2,1)S(1)}, bf16[128,768]{1,0:T(8,128)(2,1)S(1)}, u32[]{:S(2)}, u32[]{:S(2)}) collective-permute-start(bf16[128,768]{1,0:T(8,128)(2,1)S(1)} %get-tuple-element.44), channel_id=1, source_target_pairs={{0,16},{16,0},{1,17},{17,1},{2,18},{18,2},{3,19},{19,3},{4,20},{20... | collective-permute-start | bytes 589832 | tf_op jit(solution)/shard_map/ppermute | solution.py:366
  151.9 0.7 collective-permute-start.15
  152.6 2.3 %collective-permute-done.14.back_ref = bf16[128,768]{1,0:T(8,128)(2,1)S(1)} collective-permute-done((bf16[128,768]{1,0:T(8,128)(2,1)S(1)}, bf16[128,768]{1,0:T(8,128)(2,1)S(1)}, u32[]{:S(2)}, u32[]{:S(2)}) %collective-permute-start.14) | collective-permute-done | bytes 196640 | tf_op jit(solution)/shard_map/ppermute | solution.py:366
  155.0 0.8 shard_map.109
  (28 shorter events, 0.2 us)
Async XLA Ops:
  2.5 20.3 %copy-start = (bf16[1,128,1024]{2,1,0:T(8,128)(2,1)S(1)}, bf16[1,128,1024]{2,1,0:T(8,128)(2,1)}, u32[]{:S(2)}) copy-start(bf16[1,128,1024]{2,1,0:T(8,128)(2,1)} %param.12) | copy-start | bytes 786436
  2.5 25.0 %copy-start.1 = (bf16[128,768]{1,0:T(8,128)(2,1)S(1)}, bf16[128,768]{1,0:T(8,128)(2,1)}, u32[]{:S(2)}) copy-start(bf16[128,768]{1,0:T(8,128)(2,1)} %get-tuple-element.29.mine_ref.refs_2_) | copy-start | bytes 589828
  2.6 37.7 %all-to-all-start.1 = ((bf16[32,8,512]{2,1,0:T(8,128)(2,1)}), bf16[32,8,512]{2,1,0:T(8,128)(2,1)S(1)}, u32[]{:S(2)}, u32[]{:S(2)}) async-start(bf16[32,8,512]{2,1,0:T(8,128)(2,1)} %bitcast.30), calls=%async_computation.1 | async-start | bytes 524288 | tf_op jit(solution)/shard_map/all_to_all | solution.py:301
  19.7 7.9 %collective-permute-start = (bf16[128,768]{1,0:T(8,128)(2,1)}, bf16[128,768]{1,0:T(8,128)(2,1)S(1)}, u32[]{:S(2)}, u32[]{:S(2)}) collective-permute-start(bf16[128,768]{1,0:T(8,128)(2,1)} %get-tuple-element.30), channel_id=1, source_target_pairs={{0,16},{16,0},{1,17},{17,1},{2,18},{18,2},{3,19},{19,3},{4,20},{20... | collective-permute-start | bytes 589832 | tf_op jit(solution)/shard_map/ppermute | solution.py:304
  22.8 17.4 %collective-permute-start.5 = (bf16[128,1024]{1,0:T(8,128)(2,1)S(1)}, bf16[128,1024]{1,0:T(8,128)(2,1)S(1)}, u32[]{:S(2)}, u32[]{:S(2)}) collective-permute-start(bf16[128,1024]{1,0:T(8,128)(2,1)S(1)} %bitcast.25), channel_id=1, source_target_pairs={{0,16},{16,0},{1,17},{17,1},{2,18},{18,2},{3,19},{19,3},{4,20},{20... | collective-permute-start | bytes 786440 | tf_op jit(solution)/shard_map/ppermute | solution.py:305
  27.6 6.7 %copy-start.4 = (bf16[32,1024]{1,0:T(8,128)(2,1)S(1)}, bf16[32,1024]{1,0:T(8,128)(2,1)}, u32[]{:S(2)}) copy-start(bf16[32,1024]{1,0:T(8,128)(2,1)} %param.13) | copy-start | bytes 196612
  27.6 12.7 %copy-start.2 = (s32[3]{0:T(128)S(1)}, s32[3]{0:T(128)}, u32[]{:S(2)}) copy-start(s32[3]{0:T(128)} %globals_ref.5) | copy-start | bytes 40
  27.6 12.7 %collective-permute-start.1 = (bf16[2,128,512]{2,1,0:T(8,128)(2,1)S(1)}, bf16[2,128,512]{2,1,0:T(8,128)(2,1)S(1)}, u32[]{:S(2)}, u32[]{:S(2)}) collective-permute-start(bf16[2,128,512]{2,1,0:T(8,128)(2,1)S(1)} %shard_map.103), channel_id=1, source_target_pairs={{0,1},{1,2},{2,3},{3,4},{4,5},{5,6},{6,7},{7,8},{8,9},{9,10},{10,1... | collective-permute-start | bytes 786440 | tf_op jit(solution)/shard_map/ppermute | solution.py:309
  30.7 9.6 %collective-permute-start.2 = (bf16[2,128,512]{2,1,0:T(8,128)(2,1)S(1)}, bf16[2,128,512]{2,1,0:T(8,128)(2,1)S(1)}, u32[]{:S(2)}, u32[]{:S(2)}) collective-permute-start(bf16[2,128,512]{2,1,0:T(8,128)(2,1)S(1)} %shard_map.103), channel_id=1, source_target_pairs={{0,15},{1,0},{2,1},{3,2},{4,3},{5,4},{6,5},{7,6},{8,7},{9,8},{10,9... | collective-permute-start | bytes 786440 | tf_op jit(solution)/shard_map/ppermute | solution.py:310
  34.3 0.7 collective-permute-start.3
  35.0 5.3 %collective-permute-start.4 = (bf16[32,1024]{1,0:T(8,128)(2,1)S(1)}, bf16[32,1024]{1,0:T(8,128)(2,1)S(1)}, u32[]{:S(2)}, u32[]{:S(2)}) collective-permute-start(bf16[32,1024]{1,0:T(8,128)(2,1)S(1)} %collective-permute-done.3), channel_id=1, source_target_pairs={{0,64},{64,0},{128,192},{192,128},{1,65},{65,1},{129,193},{193,129... | collective-permute-start | bytes 196616 | tf_op jit(solution)/shard_map/ppermute | solution.py:307
  41.6 29.6 %all-to-all-start.2 = ((bf16[16,8,1536]{2,1,0:T(8,128)(2,1)}), bf16[16,8,1536]{2,1,0:T(8,128)(2,1)S(1)}, u32[]{:S(2)}, u32[]{:S(2)}) async-start(bf16[16,8,1536]{2,1,0:T(8,128)(2,1)} %shard_map.104), calls=%async_computation.2 | async-start | bytes 786432 | tf_op jit(solution)/shard_map/all_to_all | solution.py:280
  53.3 7.2 %collective-permute-start.6 = (bf16[64,1024]{1,0:T(8,128)(2,1)S(1)}, bf16[64,1024]{1,0:T(8,128)(2,1)S(1)}, u32[]{:S(2)}, u32[]{:S(2)}) collective-permute-start(bf16[64,1024]{1,0:T(8,128)(2,1)S(1)} %pad_maximum_fusion), channel_id=1, source_target_pairs={{0,128},{64,192},{128,0},{192,64},{1,129},{65,193},{129,1},{193,65... | collective-permute-start | bytes 393224 | tf_op jit(solution)/shard_map/ppermute | solution.py:319
  58.2 11.4 %copy-start.3 = (s32[32,3]{0,1:T(4,128)S(1)}, s32[32,3]{0,1:T(4,128)}, u32[]{:S(2)}) copy-start(s32[32,3]{0,1:T(4,128)} %param.14) | copy-start | bytes 1156
  60.6 10.2 %collective-permute-start.7 = (bf16[128,1024]{1,0:T(8,128)(2,1)S(1)}, bf16[128,1024]{1,0:T(8,128)(2,1)S(1)}, u32[]{:S(2)}, u32[]{:S(2)}) collective-permute-start(bf16[128,1024]{1,0:T(8,128)(2,1)S(1)} %constant_dynamic-update-slice_fusion.w_ref), channel_id=1, source_target_pairs={{0,32},{32,0},{1,33},{33,1},{2,34},{34,2},{3,35},{35,3},{4,36},{36... | collective-permute-start | bytes 786440 | tf_op jit(solution)/shard_map/ppermute | solution.py:323
  76.3 9.2 %collective-permute-start.10 = (bf16[4,32,1024]{2,1,0:T(8,128)(2,1)S(1)}, bf16[4,32,1024]{2,1,0:T(8,128)(2,1)S(1)}, u32[]{:S(2)}, u32[]{:S(2)}) collective-permute-start(bf16[4,32,1024]{2,1,0:T(8,128)(2,1)S(1)} %get-tuple-element.40), channel_id=1, source_target_pairs={{0,32},{32,0},{1,33},{33,1},{2,34},{34,2},{3,35},{35,3},{4,36},{36... | collective-permute-start | bytes 786440 | tf_op jit(solution)/shard_map/ppermute | solution.py:334
  85.6 11.2 %collective-permute-start.11 = (bf16[2,32,1024]{2,1,0:T(8,128)(2,1)S(1)}, bf16[2,32,1024]{2,1,0:T(8,128)(2,1)S(1)}, u32[]{:S(2)}, u32[]{:S(2)}) collective-permute-start(bf16[2,32,1024]{2,1,0:T(8,128)(2,1)S(1)} %slice.71), channel_id=1, source_target_pairs={{0,128},{64,192},{128,0},{192,64},{1,129},{65,193},{129,1},{193,65... | collective-permute-start | bytes 393224 | tf_op jit(solution)/shard_map/ppermute | solution.py:335
  90.4 25.4 %all-to-all-start.3 = ((bf16[16,8,1536]{2,1,0:T(8,128)(2,1)}), bf16[16,8,1536]{2,1,0:T(8,128)(2,1)S(1)}, u32[]{:S(2)}, u32[]{:S(2)}) async-start(bf16[16,8,1536]{2,1,0:T(8,128)(2,1)} %bitcast.7), calls=%async_computation.3 | async-start | bytes 786432 | tf_op jit(solution)/shard_map/all_to_all | solution.py:280
  96.8 5.0 %collective-permute-start.12 = (bf16[32,1024]{1,0:T(8,128)(2,1)S(1)}, bf16[32,1024]{1,0:T(8,128)(2,1)S(1)}, u32[]{:S(2)}, u32[]{:S(2)}) collective-permute-start(bf16[32,1024]{1,0:T(8,128)(2,1)S(1)} %fusion.1), channel_id=1, source_target_pairs={{0,64},{64,0},{128,192},{192,128},{1,65},{65,1},{129,193},{193,129... | collective-permute-start | bytes 196616 | tf_op jit(solution)/shard_map/ppermute | solution.py:336
  101.9 13.9 %collective-permute-start.13 = (bf16[16,1024]{1,0:T(8,128)(2,1)S(1)}, bf16[16,1024]{1,0:T(8,128)(2,1)S(1)}, u32[]{:S(2)}, u32[]{:S(2)}) collective-permute-start(bf16[16,1024]{1,0:T(8,128)(2,1)S(1)} %select_convert_fusion), channel_id=1, source_target_pairs={{0,256},{256,0},{1,257},{257,1},{2,258},{258,2},{3,259},{259,3},{4... | collective-permute-start | bytes 98312 | tf_op jit(solution)/shard_map/ppermute | solution.py:340
  117.2 27.1 %all-to-all-start.4 = ((bf16[16,8,640]{2,1,0:T(8,128)(2,1)}), bf16[16,8,640]{2,1,0:T(8,128)(2,1)S(1)}, u32[]{:S(2)}, u32[]{:S(2)}) async-start(bf16[16,8,640]{2,1,0:T(8,128)(2,1)} %get-tuple-element.41), calls=%async_computation.4 | async-start | bytes 327680 | tf_op jit(solution)/shard_map/all_to_all | solution.py:280
  128.9 13.9 %collective-permute-start.8 = (bf16[2,128,512]{2,1,0:T(8,128)(2,1)S(1)}, bf16[2,128,512]{2,1,0:T(8,128)(2,1)S(1)}, u32[]{:S(2)}, u32[]{:S(2)}) collective-permute-start(bf16[2,128,512]{2,1,0:T(8,128)(2,1)S(1)} %get-tuple-element.36), channel_id=1, source_target_pairs={{0,15},{1,0},{2,1},{3,2},{4,3},{5,4},{6,5},{7,6},{8,7},{9,8},{10,9... | collective-permute-start | bytes 786440 | tf_op jit(solution)/shard_map/ppermute | solution.py:349
  133.4 10.8 %collective-permute-start.9 = (bf16[2,128,512]{2,1,0:T(8,128)(2,1)S(1)}, bf16[2,128,512]{2,1,0:T(8,128)(2,1)S(1)}, u32[]{:S(2)}, u32[]{:S(2)}) collective-permute-start(bf16[2,128,512]{2,1,0:T(8,128)(2,1)S(1)} %get-tuple-element.37), channel_id=1, source_target_pairs={{0,1},{1,2},{2,3},{3,4},{4,5},{5,6},{6,7},{7,8},{8,9},{9,10},{10,1... | collective-permute-start | bytes 786440 | tf_op jit(solution)/shard_map/ppermute | solution.py:350
  145.0 10.0 %collective-permute-start.14 = (bf16[128,768]{1,0:T(8,128)(2,1)S(1)}, bf16[128,768]{1,0:T(8,128)(2,1)S(1)}, u32[]{:S(2)}, u32[]{:S(2)}) collective-permute-start(bf16[128,768]{1,0:T(8,128)(2,1)S(1)} %get-tuple-element.44), channel_id=1, source_target_pairs={{0,16},{16,0},{1,17},{17,1},{2,18},{18,2},{3,19},{19,3},{4,20},{20... | collective-permute-start | bytes 589832 | tf_op jit(solution)/shard_map/ppermute | solution.py:366
  151.9 0.7 collective-permute-start.15
